TPU v7x, 32 devices: a whole 2x2x4 slice. The times are simulated.
32 devices in a mesh: pages: 4 (over y, core), row: 2 (over x), col: 4 (over z).
Axes of the slice: x: 2, y: 2, z: 4, core: 2. Of those that a mesh axis runs over, the one named last changes fastest.
Arguments:
- residual: bfloat16 [128, 2, 2048], P('pages', None, ('row', 'col')), may hold values from -6 to 6
- fresh_qkv: bfloat16 [128, 2, 3, 2048], P('pages', None, None, 'col'), may hold values from -27 to 27
- prefix_pages: bfloat16 [64, 2, 128, 2048], P('pages', None, 'row', 'col'), may hold values from -6 to 6
- tail_pages: bfloat16 [128, 2, 128, 2048], P('pages', None, 'row', 'col'), may hold values from -6 to 6
- prefix_item: int32 [64], replicated, may hold values from 0 to 63, as said below
- tail_item: int32 [128], replicated, may hold values from 0 to 127, as said below
- prefix_length: int32 [8], replicated, may hold values from 1 to 1024, 5120 in all
- tail_length: int32 [128], replicated, may hold values from 1 to 128, 10240 in all
- out_weight: bfloat16 [2048, 2048], P('col', 'row'), may hold values from -0.125 to 0.125
- out_bias: bfloat16 [2048], P(('row', 'col')), may hold values from -4 to 4
- mlp_gain: bfloat16 [2048], P('row'), may hold values from 0.25 to 1.75
- mlp_shift: bfloat16 [2048], P('row'), may hold values from -4 to 4
- up_weight: bfloat16 [2048, 8192], P('row', 'col'), may hold values from -0.125 to 0.125
- up_bias: bfloat16 [8192], P(('col', 'row')), may hold values from -4 to 4
- down_weight: bfloat16 [8192, 2048], P('col', 'row'), may hold values from -0.0625 to 0.0625
- down_bias: bfloat16 [2048], P(('row', 'col')), may hold values from -4 to 4
- next_gain: bfloat16 [2048], P('row'), may hold values from 0.25 to 1.75
- next_shift: bfloat16 [2048], P('row'), may hold values from -4 to 4
- score_weight: bfloat16 [2048], P('row'), may hold values from -0.125 to 0.125
- qkv_weight: bfloat16 [2048, 6144], P('row', 'col'), may hold values from -0.125 to 0.125
- qkv_bias: bfloat16 [6144], P(('col', 'row')), may hold values from -4 to 4
Outputs:
- layer_out: bfloat16 [128, 2, 2048], P('pages', None, ('row', 'col'))
- score_out: float32 [128, 2], P('pages')
- projected_next: bfloat16 [128, 2, 6144], P('pages', None, ('col', 'row'))
Inputs may be any that keep to these rules, and one draw needn't show every extreme that they name: `prefix_item`: each of the 64 prompt pages is held by exactly one slot; slot h * 16 + g * 4 + k (k < 4) holds a page of one of the prompts g * 2 to (g + 1) * 2 - 1. `tail_item`: each continuation's tail is held by exactly one slot; slot h * 32 + g * 8 + k (k < 8) holds the tail of one of the continuations g * 32 to (g + 1) * 32 - 1. `prefix_length`: some prompt has exactly 1024 cached tokens. `tail_length`: some continuation has exactly 128 tail tokens.
All inputs are finite; a program needn't handle non-finite values.
Results may differ from a plain program's by a relative error of at most 0.023.
Values may be sent and summed in bfloat16 or wider, within the bound.
A program may use at most 64 MiB of HBM per device.

v0:
```python
import math

import jax
import jax.numpy as jnp
from jax import lax
from jax.sharding import PartitionSpec as P

D = 2048
H = 16
HD = 128
PAGE = 128
MAXPAGES = 8
CONT = 16


masked_score = -1e30
norm_eps = 1e-05


def combined_all(shard, axis, combine):
    everything = jax.tree.map(lambda part: lax.all_gather(part, axis), shard)
    first = jax.tree.map(lambda part: part[0], everything)

    def step(k, so_far):
        return combine(so_far, jax.tree.map(lambda part: part[k], everything))

    return lax.fori_loop(1, lax.axis_size(axis), step, first)


def head_slopes(first_head, how_many):
    head_index = first_head + jnp.arange(how_many, dtype=jnp.int32)
    return jnp.exp2(-8.0 * (head_index + 1).astype(jnp.float32) / H)


def slot_partials(queries, page_keys, page_values, usable, offset, slopes):
    scores = jnp.einsum(
        "sqhd,skhd->sqhk", queries, page_keys, preferred_element_type=jnp.float32
    ) / math.sqrt(HD)
    scores = scores + slopes[None, None, :, None] * offset[:, :, None, :]
    usable_full = usable[:, :, None, :]
    scores = jnp.where(usable_full, scores, masked_score)
    maxima = jnp.max(scores, axis=3)
    weights = jnp.where(usable_full, jnp.exp(scores - maxima[..., None]), 0.0)
    totals = jnp.sum(weights, axis=3)
    outputs = jnp.einsum(
        "sqhk,skhd->sqhd", weights, page_values.astype(jnp.float32), precision=lax.Precision.HIGHEST
    )
    return (maxima, totals, outputs)


def merge_pair(left_part, right_part):
    left_max, left_total, left_out = left_part
    right_max, right_total, right_out = right_part
    joined = jnp.maximum(left_max, right_max)
    left_scale = jnp.exp(left_max - joined)
    right_scale = jnp.exp(right_max - joined)
    return (
        joined,
        left_scale * left_total + right_scale * right_total,
        left_scale[..., None] * left_out + right_scale[..., None] * right_out,
    )


def fold_sources(maxima, totals, outputs):
    joined = jnp.max(maxima, axis=0)
    rescale = jnp.exp(maxima - joined[None])
    return (
        joined,
        jnp.sum(rescale * totals, axis=0),
        jnp.sum(rescale[..., None] * outputs, axis=0),
    )


def cache_partials(
    queries,
    page_block,
    page_item,
    tail_block,
    tail_owner,
    prefix_length,
    tail_length,
    row_index,
    slopes,
):
    cont_count = queries.shape[0]
    prompts = cont_count // CONT
    head_count = queries.shape[2]
    slot_count = page_block.shape[0]
    tokens = page_block.shape[2]
    token_index = row_index * tokens + jnp.arange(tokens, dtype=jnp.int32)
    step_index = jnp.arange(2, dtype=jnp.int32)
    slot_prompt = page_item // MAXPAGES
    slot_page = page_item % MAXPAGES
    by_prompt = queries.reshape(prompts, CONT * 2, head_count, HD)
    key_pos = slot_page[:, None] * PAGE + token_index[None, :]
    slot_len = prefix_length[slot_prompt]
    slot_tails = tail_length.reshape(prompts, CONT)[slot_prompt]
    query_pos = (
        slot_len[:, None, None] + slot_tails[:, :, None] + step_index[None, None, :]
    ).reshape(slot_count, CONT * 2)
    offset = (key_pos[:, None, :] - query_pos[:, :, None]).astype(jnp.float32)
    usable = jnp.broadcast_to((key_pos < slot_len[:, None])[:, None, :], offset.shape)
    page_keys = page_block[:, 0].reshape(slot_count, tokens, head_count, HD)
    page_values = page_block[:, 1].reshape(slot_count, tokens, head_count, HD)
    maxima, totals, outputs = slot_partials(
        by_prompt[slot_prompt], page_keys, page_values, usable, offset, slopes
    )
    prompt_max = (
        jnp.full((prompts, CONT * 2, head_count), masked_score, jnp.float32)
        .at[slot_prompt]
        .max(maxima)
    )
    rescale = jnp.exp(maxima - prompt_max[slot_prompt])
    prompt_total = (
        jnp.zeros((prompts, CONT * 2, head_count), jnp.float32)
        .at[slot_prompt]
        .add(rescale * totals)
    )
    prompt_out = (
        jnp.zeros((prompts, CONT * 2, head_count, HD), jnp.float32)
        .at[slot_prompt]
        .add(rescale[..., None] * outputs)
    )
    prefix_part = (
        prompt_max.reshape(cont_count, 2, head_count),
        prompt_total.reshape(cont_count, 2, head_count),
        prompt_out.reshape(cont_count, 2, head_count, HD),
    )
    tail_count = tail_block.shape[0]
    tail_lens = tail_length[tail_owner]
    tail_usable = jnp.broadcast_to(
        (token_index[None, :] < tail_lens[:, None])[:, None, :], (tail_count, 2, tokens)
    )
    tail_offset = (
        token_index[None, None, :] - tail_lens[:, None, None] - step_index[None, :, None]
    ).astype(jnp.float32)
    tail_keys = tail_block[:, 0].reshape(tail_count, tokens, head_count, HD)
    tail_values = tail_block[:, 1].reshape(tail_count, tokens, head_count, HD)
    tail_max, tail_total, tail_out = slot_partials(
        queries[tail_owner], tail_keys, tail_values, tail_usable, tail_offset, slopes
    )
    cont_max = (
        jnp.full((cont_count, 2, head_count), masked_score, jnp.float32)
        .at[tail_owner]
        .set(tail_max)
    )
    cont_total = jnp.zeros((cont_count, 2, head_count), jnp.float32).at[tail_owner].set(tail_total)
    cont_out = jnp.zeros((cont_count, 2, head_count, HD), jnp.float32).at[tail_owner].set(tail_out)
    return merge_pair(prefix_part, (cont_max, cont_total, cont_out))


def normalize(values, sum_one, sum_two, gain, shift):
    center = sum_one / D
    spread = sum_two / D - center * center
    return (
        (values - center[:, None])
        * lax.rsqrt(spread + norm_eps)[:, None]
        * gain.astype(jnp.float32)
        + shift.astype(jnp.float32)
    ).astype(jnp.bfloat16)


def shards(
    residual,
    fresh_qkv,
    prefix_pages,
    tail_pages,
    prefix_item,
    tail_item,
    prefix_length,
    tail_length,
    out_weight,
    out_bias,
    mlp_gain,
    mlp_shift,
    up_weight,
    up_bias,
    down_weight,
    down_bias,
    next_gain,
    next_shift,
    score_weight,
    qkv_weight,
    qkv_bias,
):
    group_index = lax.axis_index("pages")
    row_index = lax.axis_index("row")
    col_index = lax.axis_index("col")
    group_count = lax.axis_size("pages")
    cont_local = residual.shape[0]
    row_total = cont_local * 2
    share = residual.shape[2]
    head_count = fresh_qkv.shape[3] // HD
    slopes = head_slopes(col_index * head_count, head_count)
    fresh_rows = fresh_qkv.reshape(cont_local, 2, 3, head_count, HD)
    slot_count = prefix_pages.shape[0]
    tail_slots = tail_pages.shape[0]
    everyone = lax.all_gather(fresh_qkv[:, :, 0], "pages", axis=0, tiled=True)
    page_item = lax.dynamic_slice_in_dim(prefix_item, group_index * slot_count, slot_count)
    tail_owner = lax.dynamic_slice_in_dim(tail_item, group_index * tail_slots, tail_slots)
    maxima, totals, outputs = cache_partials(
        everyone.reshape(everyone.shape[0], 2, head_count, HD),
        prefix_pages,
        page_item,
        tail_pages,
        tail_owner,
        prefix_length,
        tail_length,
        row_index,
        slopes,
    )
    maxima, totals, outputs = (
        lax.all_to_all(
            maxima.reshape(group_count, row_total, head_count),
            "pages",
            split_axis=0,
            concat_axis=0,
            tiled=True,
        ),
        lax.all_to_all(
            totals.reshape(group_count, row_total, head_count),
            "pages",
            split_axis=0,
            concat_axis=0,
            tiled=True,
        ),
        lax.all_to_all(
            outputs.reshape(group_count, row_total, head_count, HD),
            "pages",
            split_axis=0,
            concat_axis=0,
            tiled=True,
        ),
    )
    cache_max, cache_total, cache_out = fold_sources(maxima, totals, outputs)
    cache_max, cache_total, cache_out = combined_all(
        (cache_max, cache_total, cache_out), "row", merge_pair
    )
    step_index = jnp.arange(2, dtype=jnp.int32)
    new_usable = jnp.broadcast_to(
        (step_index[None, :] <= step_index[:, None])[None], (cont_local, 2, 2)
    )
    new_offset = jnp.broadcast_to(
        (step_index[None, :] - step_index[:, None]).astype(jnp.float32)[None], (cont_local, 2, 2)
    )
    new_part = slot_partials(
        fresh_rows[:, :, 0],
        fresh_rows[:, :, 1],
        fresh_rows[:, :, 2],
        new_usable,
        new_offset,
        slopes,
    )
    joined_max, joined_total, joined_out = merge_pair(
        (
            cache_max.reshape(cont_local, 2, head_count),
            cache_total.reshape(cont_local, 2, head_count),
            cache_out.reshape(cont_local, 2, head_count, HD),
        ),
        new_part,
    )
    attended = (
        (joined_out / joined_total[..., None])
        .astype(jnp.bfloat16)
        .reshape(row_total, head_count * HD)
    )
    head_term = jnp.dot(attended, out_weight, preferred_element_type=jnp.float32)
    hidden_one = (
        residual.reshape(row_total, share).astype(jnp.float32)
        + lax.psum_scatter(head_term, "col", scatter_dimension=1, tiled=True)
        + out_bias.astype(jnp.float32)
    )
    gain_part = lax.dynamic_slice_in_dim(mlp_gain, col_index * share, share)
    shift_part = lax.dynamic_slice_in_dim(mlp_shift, col_index * share, share)
    sum_one, sum_two = lax.psum(
        (jnp.sum(hidden_one, axis=1), jnp.sum(hidden_one * hidden_one, axis=1)), ("row", "col")
    )
    normed_a = lax.all_gather(
        normalize(hidden_one, sum_one, sum_two, gain_part, shift_part), "col", axis=1, tiled=True
    )
    up_share = lax.psum_scatter(
        jnp.dot(normed_a, up_weight, preferred_element_type=jnp.float32),
        "row",
        scatter_dimension=1,
        tiled=True,
    )
    hidden_two = jax.nn.gelu(up_share + up_bias.astype(jnp.float32), approximate=True).astype(
        jnp.bfloat16
    )
    down_sum = jnp.dot(
        lax.all_gather(hidden_two, "row", axis=1, tiled=True),
        down_weight,
        preferred_element_type=jnp.float32,
    )
    down_share = lax.psum_scatter(
        down_sum.astype(jnp.bfloat16), "col", scatter_dimension=1, tiled=True
    ).astype(jnp.float32)
    layer_out = (hidden_one + down_share + down_bias.astype(jnp.float32)).astype(jnp.bfloat16)
    out_wide = layer_out.astype(jnp.float32)
    gain_part = lax.dynamic_slice_in_dim(next_gain, col_index * share, share)
    shift_part = lax.dynamic_slice_in_dim(next_shift, col_index * share, share)
    score_part = lax.dynamic_slice_in_dim(score_weight, col_index * share, share).astype(
        jnp.float32
    )
    sum_one, sum_two, score_sum = lax.psum(
        (
            jnp.sum(out_wide, axis=1),
            jnp.sum(out_wide * out_wide, axis=1),
            jnp.sum(out_wide * score_part, axis=1),
        ),
        ("row", "col"),
    )
    normed_b = lax.all_gather(
        normalize(out_wide, sum_one, sum_two, gain_part, shift_part), "col", axis=1, tiled=True
    )
    qkv_share = lax.psum_scatter(
        jnp.dot(normed_b, qkv_weight, preferred_element_type=jnp.float32).astype(jnp.bfloat16),
        "row",
        scatter_dimension=1,
        tiled=True,
    ).astype(jnp.float32)
    projected_next = (qkv_share + qkv_bias.astype(jnp.float32)).astype(jnp.bfloat16)
    return (
        layer_out.reshape(cont_local, 2, share),
        score_sum.reshape(cont_local, 2),
        projected_next.reshape(cont_local, 2, qkv_share.shape[1]),
    )


def solution(mesh):
    in_specs = (
        P("pages", None, ("row", "col")),
        P("pages", None, None, "col"),
        P("pages", None, "row", "col"),
        P("pages", None, "row", "col"),
        P(),
        P(),
        P(),
        P(),
        P("col", "row"),
        P(("row", "col")),
        P("row"),
        P("row"),
        P("row", "col"),
        P(("col", "row")),
        P("col", "row"),
        P(("row", "col")),
        P("row"),
        P("row"),
        P("row"),
        P("row", "col"),
        P(("col", "row")),
    )
    out_specs = (
        P("pages", None, ("row", "col")),
        P("pages", None),
        P("pages", None, ("col", "row")),
    )
    return jax.shard_map(shards, mesh=mesh, in_specs=in_specs, out_specs=out_specs, check_vma=False)
```

profile of v0, /device:TPU:0, one launch (start us, length us, event | category | flops | bytes accessed | tf_op | source)
XLA Modules:
  0.0 302.5 jit_solution(9328350891376823541)
XLA Ops:
  8.2 7.2 %all-gather = bf16[128,2,1,512]{3,1,2,0:T(2,128)(2,1)S(1)} all-gather(bf16[32,2,1,512]{3,1,2,0:T(2,128)(2,1)S(1)} %slice.36), channel_id=2, replica_groups=mesh['pages'=4,'row'=2,'col'=4] {'pages'}, dimensions={0}, use_global_device_ids=true | all-gather | bytes 327680 | tf_op jit(solution)/shard_map/all_gather | solution.py:198
  19.3 1.4 gather_fusion.3
  21.6 3.1 %fusion.70 = (bf16[16,1,64,512]{3,2,1,0:T(8,128)(2,1)}, bf16[16,1,64,512]{3,2,1,0:T(8,128)(2,1)}) fusion(bf16[16,2,64,512]{3,2,1,0:T(8,128)(2,1)} %param.23), kind=kLoop, calls=%fused_computation.137 | loop fusion | bytes 4194304 | tf_op jit(solution)/shard_map/slice | solution.py:103
  27.5 1.4 gather_fusion.1
  28.9 2.2 reshape_squeeze.12
  31.3 3.0 %fusion.76 = (f32[16,32,4]{1,2,0:T(4,128)S(1)}, f32[16,32,4,64]{3,1,2,0:T(8,128)}) fusion(f32[16,32,64]{2,1,0:T(8,128)S(1)} %subtract_convert_fusion, f32[4]{0:T(128)S(1)} %multiply_exponential_fusion, bf16[16,32,4,128]{3,1,2,0:T(8,128)(2,1)} %gather_fusion.1, bf16[16,64,4,128]{3,2,1,0:T(4,128)(2,1)} %reshape_squeeze.12, ...), kind=kOutput, calls=%fused_computation.143 | convolution fusion | flops 34207744 | bytes 2237456 | tf_op jit(solution)/shard_map/sqhd,skhd->sqhk/dot_general | solution.py:36
  34.3 1.1 scatter_fusion
  36.8 1.9 fusion.28
  38.7 4.7 %fusion.69 = (bf16[32,1,64,512]{3,2,1,0:T(8,128)(2,1)}, bf16[32,1,64,512]{3,2,1,0:T(8,128)(2,1)}) fusion(bf16[32,2,64,512]{3,2,1,0:T(8,128)(2,1)} %param.24), kind=kLoop, calls=%fused_computation.136 | loop fusion | bytes 8388608 | tf_op jit(solution)/shard_map/slice | solution.py:137
  43.5 4.0 %reshape_squeeze.13 = bf16[32,64,4,128]{3,2,1,0:T(4,128)(2,1)} reshape(bf16[32,1,64,512]{3,2,1,0:T(8,128)(2,1)} %get-tuple-element.72) | data formatting | bytes 4194304 | tf_op jit(solution)/shard_map/reshape;squeeze | solution.py:137
  47.4 1.6 gather_fusion.4
  49.0 2.9 fusion.77
  54.2 1.2 scatter_fusion.4
  56.3 2.6 scatter_fusion.5
  59.0 2.6 scatter_fusion.1
  61.5 1.8 multiply_add_fusion
  65.0 4.0 %all-to-all-start = ((f32[4,1,256]{2,1,0:T(1,128)}), f32[4,1,256]{2,1,0:T(1,128)}, u32[]{:S(2)}, u32[]{:S(2)}) async-start(f32[4,1,256]{2,1,0:T(1,128)} %reshape.438), calls=%async_computation | async-start | bytes 8192 | tf_op jit(solution)/shard_map/all_to_all | solution.py:213
  71.9 2.1 reshape_squeeze.14
  74.0 3.7 %fusion.4 = f32[16,32,4,128]{3,1,2,0:T(8,128)} fusion(bf16[16,64,4,128]{3,2,1,0:T(4,128)(2,1)} %reshape_squeeze.14, f32[16,32,4,64]{3,1,2,0:T(8,128)} %get-tuple-element.92, f32[16,32,4]{1,2,0:T(4,128)S(1)} %get-tuple-element.91, f32[16,32,4]{1,2,0:T(4,128)S(1)} %bitcast.134, pred[16,64]{1,0:T(8,128)(4,1)S(1)} %copy-done.13), kind=kOutput, calls=%fused_computation.18 | convolution fusion | flops 201850880 | bytes 2638848 | tf_op jit(solution)/shard_map/sqhk,skhd->sqhd/dot_general | solution.py:45
  78.6 3.7 %scatter_fusion.2 = f32[8,32,4,128]{3,1,2,0:T(8,128)} fusion(f32[8,32,4,128]{3,1,2,0:T(8,128)} %broadcast_in_dim.86, s32[16]{0:T(128)S(1)} %copy-done.17, f32[16,32,4,128]{3,1,2,0:T(8,128)} %fusion.4), kind=kCustom, calls=%fused_computation.8 | custom fusion | flops 262144 | bytes 3145792 | tf_op jit(solution)/shard_map/scatter-add | solution.py:122
  82.3 1.9 copy.182
  84.1 4.0 %reshape_squeeze.15 = bf16[32,64,4,128]{3,2,1,0:T(4,128)(2,1)} reshape(bf16[32,1,64,512]{3,2,1,0:T(8,128)(2,1)} %get-tuple-element.73) | data formatting | bytes 4194304 | tf_op jit(solution)/shard_map/reshape;squeeze | solution.py:138
  88.2 3.4 %fusion.8 = f32[32,2,4,128]{3,1,2,0:T(2,128)S(1)} fusion(bf16[32,64,4,128]{3,2,1,0:T(4,128)(2,1)} %reshape_squeeze.15, f32[32,2,4,64]{3,1,2,0:T(2,128)S(1)} %copy-done.10, pred[32,64]{1,0:T(8,128)(4,1)S(1)} %copy-done.15, f32[32,2,4]{1,2,0:T(4,128)S(1)} %get-tuple-element.93), kind=kOutput, calls=%fused_computation.24 | convolution fusion | flops 25198592 | bytes 2296832 | tf_op jit(solution)/shard_map/sqhk,skhd->sqhd/dot_general | solution.py:45
  92.5 3.5 %scatter_fusion.3 = f32[128,2,4,128]{3,2,1,0:T(4,128)} fusion(f32[128,2,4,128]{3,2,1,0:T(4,128)} %broadcast_in_dim.88, s32[32]{0:T(128)S(1)} %copy-done.19, f32[32,2,4,128]{3,2,1,0:T(4,128)S(1)} %copy.185), kind=kCustom, calls=%fused_computation.9 | custom fusion | bytes 393344 | tf_op jit(solution)/shard_map/scatter | solution.py:148
  96.1 1.3 fusion.75
  97.4 2.2 fusion.56
  99.6 1.5 fusion.29
  103.2 3.3 %all-to-all-start.2 = ((f32[4,1,256]{2,1,0:T(1,128)}), f32[4,1,256]{2,1,0:T(1,128)S(1)}, u32[]{:S(2)}, u32[]{:S(2)}) async-start(f32[4,1,256]{2,1,0:T(1,128)} %reshape.440), calls=%async_computation.2 | async-start | bytes 8192 | tf_op jit(solution)/shard_map/all_to_all | solution.py:220
  107.0 1.3 reduce
  108.5 1.8 all-to-all-done.2
  110.3 4.1 %all-to-all-start.1 = ((f32[4,64,4,128]{3,2,1,0:T(4,128)}), f32[4,64,4,128]{3,2,1,0:T(4,128)}, u32[]{:S(2)}, u32[]{:S(2)}) async-start(f32[4,64,4,128]{3,2,1,0:T(4,128)} %bitcast.121), calls=%async_computation.1 | async-start | bytes 1048576 | tf_op jit(solution)/shard_map/all_to_all | solution.py:227
  115.4 4.3 %all-gather.5 = f32[2,64,4]{1,2,0:T(4,128)S(1)} all-gather(f32[1,64,4]{1,2,0:T(4,128)S(1)} %bitcast.155), channel_id=5, replica_groups=mesh['pages'=4,'row'=2,'col'=4] {'row'}, dimensions={0}, use_global_device_ids=true | all-gather | bytes 3072 | tf_op jit(solution)/shard_map/all_gather | solution.py:21
  120.1 4.3 %all-gather.4 = f32[2,64,4]{1,2,0:T(4,128)S(1)} all-gather(f32[1,64,4]{1,2,0:T(4,128)S(1)} %bitcast.143), channel_id=3, replica_groups=mesh['pages'=4,'row'=2,'col'=4] {'row'}, dimensions={0}, use_global_device_ids=true | all-gather | bytes 3072 | tf_op jit(solution)/shard_map/all_gather | solution.py:21
  124.9 1.5 multiply_reduce_fusion
  126.4 5.6 %all-gather.2 = f32[128,4,128]{2,1,0:T(4,128)S(1)} all-gather(f32[64,4,128]{2,1,0:T(4,128)S(1)} %multiply_reduce_fusion), channel_id=4, replica_groups=mesh['pages'=4,'row'=2,'col'=4] {'row'}, dimensions={0}, use_global_device_ids=true | all-gather | bytes 393216 | tf_op jit(solution)/shard_map/all_gather | solution.py:21
  132.1 1.1 fusion.43
  135.2 20.6 %reduce-scatter.5.cloned.1.call-done = f32[64,256]{1,0:T(8,128)} async-done(((f32[64,1024]{1,0:T(8,128)}), f32[64,256]{1,0:T(8,128)}) %reduce-scatter.5.cloned.1.call-update) | async-done | bytes 65552 | tf_op jit(solution)/shard_map/reduce_scatter | solution.py:270
  156.8 18.7 %all-reduce.1 = (f32[64]{0:T(128)S(1)}, f32[64]{0:T(128)S(1)}) all-reduce(f32[64]{0:T(128)S(1)} %get-tuple-element.46, f32[64]{0:T(128)S(1)} %get-tuple-element.45), channel_id=1, replica_groups=mesh['pages'=4,'row'=2,'col'=4] {'row','col'}, use_global_device_ids=true, to_apply=%region_19.20 | all-reduce | flops 128 | bytes 1024 | tf_op jit(solution)/shard_map/psum | solution.py:275
  175.5 13.3 %all_gather.37 = bf16[64,1024]{1,0:T(8,128)(2,1)S(1)} all-gather(bf16[64,256]{1,0:T(8,128)(2,1)S(1)} %add_convert_fusion.2), channel_id=1, replica_groups=mesh['pages'=4,'row'=2,'col'=4] {'col'}, dimensions={1}, use_global_device_ids=true | all-gather | bytes 163840 | tf_op jit(solution)/shard_map/all_gather | solution.py:278
  188.9 3.8 %fusion.78 = f32[64,2048]{1,0:T(8,128)} fusion(bf16[64,1024]{1,0:T(8,128)(2,1)S(1)} %all_gather.37, bf16[1024,2048]{1,0:T(8,128)(2,1)} %param.33), kind=kOutput, calls=%fused_computation.146 | convolution fusion | flops 268435456 | bytes 4849664 | tf_op jit(solution)/shard_map/dot_general | solution.py:282
  192.8 12.8 %reduce-scatter.7.cloned.1.call-done = f32[64,1024]{1,0:T(8,128)} async-done(((f32[64,2048]{1,0:T(8,128)}), f32[64,1024]{1,0:T(8,128)}) %reduce-scatter.7.cloned.1.call-update) | async-done | bytes 262160 | tf_op jit(solution)/shard_map/reduce_scatter | solution.py:281
  206.7 5.9 %all_gather.38 = bf16[64,2048]{1,0:T(8,128)(2,1)S(1)} all-gather(bf16[64,1024]{1,0:T(8,128)(2,1)S(1)} %fusion.40), channel_id=1, replica_groups=mesh['pages'=4,'row'=2,'col'=4] {'row'}, dimensions={1}, use_global_device_ids=true | all-gather | bytes 393216 | tf_op jit(solution)/shard_map/all_gather | solution.py:291
  212.6 3.7 %convolution_convert_fusion.1 = bf16[64,1024]{1,0:T(8,128)(2,1)} fusion(bf16[64,2048]{1,0:T(8,128)(2,1)S(1)} %all_gather.38, bf16[2048,1024]{1,0:T(8,128)(2,1)} %param.35), kind=kOutput, calls=%fused_computation.23 | convolution fusion | flops 268500992 | bytes 4587520 | tf_op jit(solution)/shard_map/dot_general | solution.py:290
  217.9 17.7 %reduce-scatter.9.cloned.1.call-done = bf16[64,256]{1,0:T(8,128)(2,1)} async-done(((bf16[64,1024]{1,0:T(8,128)(2,1)}), bf16[64,256]{1,0:T(8,128)(2,1)}) %reduce-scatter.9.cloned.1.call-update) | async-done | bytes 32784 | tf_op jit(solution)/shard_map/reduce_scatter | solution.py:295
  236.7 34.5 %all-reduce = (f32[32,2]{1,0:T(8,128)S(1)}, f32[64]{0:T(128)S(1)}, f32[64]{0:T(128)S(1)}) all-reduce(f32[32,2]{1,0:T(8,128)S(1)} %reshape.296, f32[64]{0:T(128)S(1)} %get-tuple-element.48, f32[64]{0:T(128)S(1)} %get-tuple-element.47), channel_id=1, replica_groups=mesh['pages'=4,'row'=2,'col'=4] {'row','col'}, use_global_device_ids=true, to_apply=%region_23.24 | all-reduce | flops 192 | bytes 1536 | tf_op jit(solution)/shard_map/psum | solution.py:305
  271.3 13.4 %all_gather.39 = bf16[64,1024]{1,0:T(8,128)(2,1)S(1)} all-gather(bf16[64,256]{1,0:T(8,128)(2,1)S(1)} %fusion.50), channel_id=1, replica_groups=mesh['pages'=4,'row'=2,'col'=4] {'col'}, dimensions={1}, use_global_device_ids=true | all-gather | bytes 163840 | tf_op jit(solution)/shard_map/all_gather | solution.py:313
  284.7 1.3 convolution_convert_fusion
  287.3 7.1 %reduce-scatter.11.cloned.1.call-done = bf16[64,768]{1,0:T(8,128)(2,1)} async-done(((bf16[64,1536]{1,0:T(8,128)(2,1)}), bf16[64,768]{1,0:T(8,128)(2,1)}) %reduce-scatter.11.cloned.1.call-update) | async-done | bytes 98320 | tf_op jit(solution)/shard_map/reduce_scatter | solution.py:316
  (165 shorter events, 33.7 us)
Async XLA Ops:
  7.2 277.5 %copy-start = (bf16[1024,1536]{1,0:T(8,128)(2,1)S(1)}, bf16[1024,1536]{1,0:T(8,128)(2,1)}, u32[]{:S(2)}) copy-start(bf16[1024,1536]{1,0:T(8,128)(2,1)} %param.40) | copy-start | bytes 9437188
  7.2 14.2 %copy-start.22 = (s32[64]{0:T(128)S(1)}, s32[64]{0:T(128)}, u32[]{:S(2)}) copy-start(s32[64]{0:T(128)} %param.25) | copy-start | bytes 772
  18.7 0.6 copy-start.18
  21.4 9.9 %copy-start.27 = (f32[4]{0:T(128)}, f32[4]{0:T(128)S(1)}, u32[]{:S(2)}) copy-start(f32[4]{0:T(128)S(1)} %multiply_exponential_fusion) | copy-start | bytes 52
  21.6 12.8 %copy-start.16 = (s32[16]{0:T(128)}, s32[16]{0:T(128)S(1)}, u32[]{:S(2)}) copy-start(s32[16]{0:T(128)S(1)} %compare_select_fusion.1) | copy-start | bytes 196
  21.6 3.7 %copy-start.1 = (s32[8]{0:T(128)S(1)}, s32[8]{0:T(128)}, u32[]{:S(2)}) copy-start(s32[8]{0:T(128)} %param.27) | copy-start | bytes 100
  26.1 10.7 %copy-start.12 = (pred[16,64]{1,0:T(8,128)(4,1)}, pred[16,64]{1,0:T(8,128)(4,1)S(1)}, u32[]{:S(2)}) copy-start(pred[16,64]{1,0:T(8,128)(4,1)S(1)} %broadcast_compare_fusion.1) | copy-start | bytes 3076
  43.4 5.6 %copy-start.14 = (pred[32,64]{1,0:T(8,128)(4,1)S(1)}, pred[32,64]{1,0:T(8,128)(4,1)}, u32[]{:S(2)}) copy-start(pred[32,64]{1,0:T(8,128)(4,1)} %broadcast_compare_fusion) | copy-start | bytes 6148
  43.5 5.6 %copy-start.28 = (f32[4]{0:T(128)S(1)}, f32[4]{0:T(128)}, u32[]{:S(2)}) copy-start(f32[4]{0:T(128)} %copy-done.27) | copy-start | bytes 52
  51.9 3.5 %copy-start.9 = (f32[32,2,4,64]{3,1,2,0:T(2,128)}, f32[32,2,4,64]{3,1,2,0:T(2,128)S(1)}, u32[]{:S(2)}) copy-start(f32[32,2,4,64]{3,1,2,0:T(2,128)S(1)} %get-tuple-element.94) | copy-start | bytes 196612
  58.9 15.1 %copy-start.13 = (pred[16,64]{1,0:T(8,128)(4,1)S(1)}, pred[16,64]{1,0:T(8,128)(4,1)}, u32[]{:S(2)}) copy-start(pred[16,64]{1,0:T(8,128)(4,1)} %copy-done.12) | copy-start | bytes 3076
  65.0 38.2 %all-to-all-start = ((f32[4,1,256]{2,1,0:T(1,128)}), f32[4,1,256]{2,1,0:T(1,128)}, u32[]{:S(2)}, u32[]{:S(2)}) async-start(f32[4,1,256]{2,1,0:T(1,128)} %reshape.438), calls=%async_computation | async-start | bytes 8192 | tf_op jit(solution)/shard_map/all_to_all | solution.py:213
  74.0 4.6 %copy-start.17 = (s32[16]{0:T(128)S(1)}, s32[16]{0:T(128)}, u32[]{:S(2)}) copy-start(s32[16]{0:T(128)} %copy-done.16) | copy-start | bytes 196
  84.1 4.0 %copy-start.10 = (f32[32,2,4,64]{3,1,2,0:T(2,128)S(1)}, f32[32,2,4,64]{3,1,2,0:T(2,128)}, u32[]{:S(2)}) copy-start(f32[32,2,4,64]{3,1,2,0:T(2,128)} %copy-done.9) | copy-start | bytes 196612
  84.1 4.0 %copy-start.15 = (pred[32,64]{1,0:T(8,128)(4,1)S(1)}, pred[32,64]{1,0:T(8,128)(4,1)}, u32[]{:S(2)}) copy-start(pred[32,64]{1,0:T(8,128)(4,1)} %broadcast_compare_fusion) | copy-start | bytes 6148
  88.2 4.4 %copy-start.19 = (s32[32]{0:T(128)S(1)}, s32[32]{0:T(128)}, u32[]{:S(2)}) copy-start(s32[32]{0:T(128)} %copy-done.18) | copy-start | bytes 388
  88.2 7.9 %copy-start.23 = (pred[2,2]{0,1:T(4,128)(4,1)S(1)}, pred[2,2]{0,1:T(4,128)(4,1)}, u32[]{:S(2)}) copy-start(pred[2,2]{0,1:T(4,128)(4,1)} %iota_compare_fusion) | copy-start | bytes 16
  88.2 7.9 %copy-start.26 = (f32[2,2]{0,1:T(2,128)S(1)}, f32[2,2]{0,1:T(2,128)}, u32[]{:S(2)}) copy-start(f32[2,2]{0,1:T(2,128)} %subtract_convert_fusion.2) | copy-start | bytes 52
  88.2 7.9 %copy-start.29 = (f32[4]{0:T(128)S(1)}, f32[4]{0:T(128)}, u32[]{:S(2)}) copy-start(f32[4]{0:T(128)} %copy-done.27) | copy-start | bytes 52
  91.6 8.0 %copy-start.5 = (f32[32,8,4]{2,1,0:T(8,128)S(1)}, f32[32,8,4]{2,1,0:T(8,128)}, u32[]{:S(2)}) copy-start(f32[32,8,4]{2,1,0:T(8,128)} %get-tuple-element.102) | copy-start | bytes 12292
  91.6 8.0 %copy-start.6 = (f32[32,8,4]{2,1,0:T(8,128)S(1)}, f32[32,8,4]{2,1,0:T(8,128)}, u32[]{:S(2)}) copy-start(f32[32,8,4]{2,1,0:T(8,128)} %get-tuple-element.103) | copy-start | bytes 12292
  96.0 3.6 %copy-start.2 = (f32[128,2,4,128]{3,2,1,0:T(4,128)S(1)}, f32[128,2,4,128]{3,2,1,0:T(4,128)}, u32[]{:S(2)}) copy-start(f32[128,2,4,128]{3,2,1,0:T(4,128)} %scatter_fusion.3) | copy-start | bytes 1572868
  96.0 3.6 %copy-start.3 = (f32[8,32,4,128]{3,1,0,2:T(8,128)S(1)}, f32[8,32,4,128]{3,1,0,2:T(8,128)}, u32[]{:S(2)}) copy-start(f32[8,32,4,128]{3,1,0,2:T(8,128)} %copy.182) | copy-start | bytes 1572868
  96.0 6.3 %copy-start.7 = (f32[32,8,4]{2,1,0:T(8,128)S(1)}, f32[32,8,4]{2,1,0:T(8,128)}, u32[]{:S(2)}) copy-start(f32[32,8,4]{2,1,0:T(8,128)} %get-tuple-element.101) | copy-start | bytes 12292
  97.4 3.8 %copy-start.8 = (f32[32,2,4]{1,2,0:T(4,128)}, f32[32,2,4]{1,2,0:T(4,128)S(1)}, u32[]{:S(2)}) copy-start(f32[32,2,4]{1,2,0:T(4,128)S(1)} %get-tuple-element.89) | copy-start | bytes 3076
  103.2 7.0 %all-to-all-start.2 = ((f32[4,1,256]{2,1,0:T(1,128)}), f32[4,1,256]{2,1,0:T(1,128)S(1)}, u32[]{:S(2)}, u32[]{:S(2)}) async-start(f32[4,1,256]{2,1,0:T(1,128)} %reshape.440), calls=%async_computation.2 | async-start | bytes 8192 | tf_op jit(solution)/shard_map/all_to_all | solution.py:220
  110.3 14.6 %all-to-all-start.1 = ((f32[4,64,4,128]{3,2,1,0:T(4,128)}), f32[4,64,4,128]{3,2,1,0:T(4,128)}, u32[]{:S(2)}, u32[]{:S(2)}) async-start(f32[4,64,4,128]{3,2,1,0:T(4,128)} %bitcast.121), calls=%async_computation.1 | async-start | bytes 1048576 | tf_op jit(solution)/shard_map/all_to_all | solution.py:227
  114.4 41.4 %reduce-scatter.5.cloned.1.call-start = ((), (), s32[]{:S(2)}) async-start(), calls=%async_computation.7 | async-start | bytes 327680 | tf_op jit(solution)/shard_map/reduce_scatter | solution.py:270
  124.8 9.5 %copy-start.24 = (bf16[256]{0:T(256)(128)(2,1)S(1)}, bf16[256]{0:T(256)(128)(2,1)}, u32[]{:S(2)}) copy-start(bf16[256]{0:T(256)(128)(2,1)} %param.30) | copy-start | bytes 1540
  124.8 9.5 %copy-start.11 = (bf16[32,2,256]{2,1,0:T(2,128)(2,1)S(1)}, bf16[32,2,256]{2,1,0:T(2,128)(2,1)}, u32[]{:S(2)}) copy-start(bf16[32,2,256]{2,1,0:T(2,128)(2,1)} %param.21) | copy-start | bytes 98308
  124.8 8.4 %copy-start.4 = (bf16[512,1024]{1,0:T(8,128)(2,1)S(1)}, bf16[512,1024]{1,0:T(8,128)(2,1)}, u32[]{:S(2)}) copy-start(bf16[512,1024]{1,0:T(8,128)(2,1)} %param.29) | copy-start | bytes 3145732
  134.3 71.4 %reduce-scatter.7.cloned.1.call-start = ((), (), s32[]{:S(2)}) async-start(), calls=%async_computation.8 | async-start | bytes 786432 | tf_op jit(solution)/shard_map/reduce_scatter | solution.py:281
  188.9 3.9 %copy-start.20 = (bf16[1024]{0:T(1024)(128)(2,1)S(1)}, bf16[1024]{0:T(1024)(128)(2,1)}, u32[]{:S(2)}) copy-start(bf16[1024]{0:T(1024)(128)(2,1)} %param.34) | copy-start | bytes 6148
  192.8 42.9 %reduce-scatter.9.cloned.1.call-start = ((), (), s32[]{:S(2)}) async-start(), calls=%async_computation.9 | async-start | bytes 163840 | tf_op jit(solution)/shard_map/reduce_scatter | solution.py:295
  212.6 3.8 %copy-start.25 = (bf16[256]{0:T(256)(128)(2,1)S(1)}, bf16[256]{0:T(256)(128)(2,1)}, u32[]{:S(2)}) copy-start(bf16[256]{0:T(256)(128)(2,1)} %param.36) | copy-start | bytes 1540
  216.3 69.7 %copy-start.21 = (bf16[768]{0:T(1024)(128)(2,1)S(1)}, bf16[768]{0:T(1024)(128)(2,1)}, u32[]{:S(2)}) copy-start(bf16[768]{0:T(1024)(128)(2,1)} %param.41) | copy-start | bytes 4612
  216.3 78.1 %reduce-scatter.11.cloned.1.call-start = ((), (), s32[]{:S(2)}) async-start(), calls=%async_computation.10 | async-start | bytes 294912 | tf_op jit(solution)/shard_map/reduce_scatter | solution.py:316
Sparse Core Ops, SparseCore 0:
  134.4 21.3 reduce-scatter.4
  192.9 12.7 reduce-scatter.6
  216.4 19.1 reduce-scatter.8
  286.2 8.1 reduce-scatter.10
where the time goes:
time: 304 us; the launch traced here: 303 us
  blocking collectives  107 us (35%)
  waiting for transfers between devices  60.1 us (20%)
  local copies, waits for them, and re-layouts  56.5 us (19%)
  matrix products  26.4 us (9%)
  other arithmetic  26.2 us (9%)
  between operations  14.4 us (5%)
  starting transfers between devices  11.5 us (4%)
    psum x1, blocking collectives, shards(): lax.psum((jnp.sum(out_wide, axis=1), jnp.sum(out_wide * out_wide, axis=1)...  34.5 us
    reduce_scatter x1, waiting for transfers between devices, shards(): lax.psum_scatter(head_term, 'col', scatter_dimension=1, tiled=True)  20.6 us
    psum x1, blocking collectives, shards(): lax.psum((jnp.sum(hidden_one, axis=1), jnp.sum(hidden_one * hidden_one, a...  18.7 us
    reduce_scatter x1, waiting for transfers between devices, shards(): lax.psum_scatter(down_sum.astype(jnp.bfloat16), 'col', scatter_dimension=...  17.7 us
    all_gather x3, blocking collectives, combined_all(): everything = jax.tree.map(lambda part: lax.all_gather(part, axis), shard)  14.3 us
    all_gather x1, blocking collectives, shards(): lax.all_gather(normalize(out_wide, sum_one, sum_two, gain_part, shift_par...  13.4 us
    all_gather x1, blocking collectives, shards(): lax.all_gather(normalize(hidden_one, sum_one, sum_two, gain_part, shift_p...  13.3 us
    reduce_scatter x1, waiting for transfers between devices, shards(): lax.psum_scatter(jnp.dot(normed_a, up_weight, preferred_element_type=jnp....  12.8 us
  transfers between devices with their start and end apart: 7, of which 5 were waited for; matrix products, arithmetic and copies ran while one was open for 14% of the time, Pallas kernels for 0%

commit v1 on v0

--- a/solution.py
+++ b/solution.py
@@ -3,6 +3,8 @@
 import jax
 import jax.numpy as jnp
 from jax import lax
+from jax.experimental import pallas as pl
+from jax.experimental.pallas import tpu as pltpu
 from jax.sharding import PartitionSpec as P
 
 D = 2048
@@ -160,7 +162,7 @@
     ).astype(jnp.bfloat16)
 
 
-def shards(
+def plain_shards(
     residual,
     fresh_qkv,
     prefix_pages,
@@ -327,6 +329,738 @@
     )
 
 
+empty_floor = -1e20
+STAT = 8
+LANES = 128
+
+
+def columns_to_tile(columns):
+    rows = columns[0].shape[0]
+    lane = lax.broadcasted_iota(jnp.int32, (rows, LANES), 1)
+    wide = jnp.zeros((rows, LANES), jnp.float32)
+    for k, column in enumerate(columns):
+        wide = jnp.where(lane == k, column, wide)
+    if rows < LANES:
+        wide = jnp.concatenate([wide, jnp.zeros((LANES - rows, LANES), jnp.float32)], axis=0)
+    return jnp.transpose(wide)[:STAT]
+
+
+def tile_to_columns(tile, rows):
+    have = tile.shape[0]
+    if have < LANES:
+        tile = jnp.concatenate([tile, jnp.zeros((LANES - have, LANES), jnp.float32)], axis=0)
+    return jnp.transpose(tile)[:rows]
+
+
+def layer_kernel(
+    sizes,
+    prefix_item,
+    tail_item,
+    prefix_length,
+    tail_length,
+    tail_row,
+    fresh,
+    residual,
+    vectors,
+    prefix_hbm,
+    tail_hbm,
+    out_hbm,
+    up_hbm,
+    down_hbm,
+    qkv_hbm,
+    layer_ref,
+    stat_ref,
+    proj_ref,
+    prefix_v,
+    tail_v,
+    out_w,
+    up_w,
+    down_w,
+    qkv_w,
+    q_buf,
+    p_stage,
+    l_stage,
+    p_buf,
+    l_buf,
+    att,
+    a_stage,
+    a_buf,
+    hidden,
+    x_buf,
+    s_buf,
+    normed,
+    u_own,
+    u_stage,
+    u_buf,
+    acc,
+    d_stage,
+    d_buf,
+    y_buf,
+    t_buf,
+    z_stage,
+    z_buf,
+    page_sem,
+    w_sem,
+    q_send,
+    q_recv,
+    p_send,
+    p_recv,
+    l_send,
+    l_recv,
+    a_send,
+    a_recv,
+    x_send,
+    x_recv,
+    s_send,
+    s_recv,
+    u_send,
+    u_recv,
+    d_send,
+    d_recv,
+    y_send,
+    y_recv,
+    t_send,
+    t_recv,
+    z_send,
+    z_recv,
+):
+    G, R, C = sizes["pages"], sizes["row"], sizes["col"]
+    f32, bf16, i32 = jnp.float32, jnp.bfloat16, jnp.int32
+    me = lax.axis_index("pages")
+    row = lax.axis_index("row")
+    col = lax.axis_index("col")
+    rows = residual.shape[0]
+    share = residual.shape[1]
+    width = C * share
+    heads = fresh.shape[2] // HD
+    slots, _, tokens, _ = prefix_v.shape
+    tails = tail_v.shape[0]
+    pair_pages, pair_tails = slots // G, tails // G
+    chunks, _, chunk = u_buf.shape
+    pieces, _, piece = z_buf.shape
+
+    def group_at(i):
+        return lax.rem(lax.div(me, 2) + lax.div(i, 2), G // 2) * 2 + lax.rem(me + i, 2)
+
+    def row_at(k):
+        return lax.rem(row + k, R)
+
+    def col_at(k):
+        return lax.rem(col + k, C)
+
+    def remote(src, dst, send_sem, recv_sem, target):
+        return pltpu.make_async_remote_copy(
+            src_ref=src,
+            dst_ref=dst,
+            send_sem=send_sem,
+            recv_sem=recv_sem,
+            device_id=target,
+            device_id_type=pl.DeviceIdType.MESH,
+        )
+
+    def prefix_copy(g):
+        part = pl.ds(g * pair_pages, pair_pages)
+        return pltpu.make_async_copy(prefix_hbm.at[part], prefix_v.at[part], page_sem.at[g, 0])
+
+    def tail_copy(g):
+        part = pl.ds(g * pair_tails, pair_tails)
+        return pltpu.make_async_copy(tail_hbm.at[part], tail_v.at[part], page_sem.at[g, 1])
+
+    weight_copies = [
+        pltpu.make_async_copy(src, dst, w_sem.at[k])
+        for k, (src, dst) in enumerate(
+            ((out_hbm, out_w), (up_hbm, up_w), (down_hbm, down_w), (qkv_hbm, qkv_w))
+        )
+    ]
+
+    for i in range(G):
+        prefix_copy(group_at(jnp.int32(i))).start()
+        tail_copy(group_at(jnp.int32(i))).start()
+
+    barrier = pltpu.get_barrier_semaphore()
+    met = 0
+    for i in range(G):
+        for k in range(R):
+            if i or k:
+                met += 1
+                pl.semaphore_signal(
+                    barrier,
+                    inc=1,
+                    device_id=(group_at(jnp.int32(i)), row_at(k), col),
+                    device_id_type=pl.DeviceIdType.MESH,
+                )
+    for k in range(R):
+        for j in range(1, C):
+            met += 1
+            pl.semaphore_signal(
+                barrier,
+                inc=1,
+                device_id=(me, row_at(k), col_at(j)),
+                device_id_type=pl.DeviceIdType.MESH,
+            )
+    pl.semaphore_wait(barrier, met)
+
+    sends = []
+    for i in range(1, G):
+        copy = remote(
+            fresh.at[0],
+            q_buf.at[me],
+            q_send.at[i],
+            q_recv.at[me],
+            (group_at(jnp.int32(i)), row, col),
+        )
+        copy.start()
+        sends.append(copy)
+    q_buf[me] = fresh[0]
+    for copy in weight_copies:
+        copy.start()
+
+    row_id = lax.broadcasted_iota(i32, (rows, 1), 0)
+    step = lax.rem(row_id, 2)
+    row_cont = lax.div(row_id, 2)
+    contract_last = (((1,), (1,)), ((), ()))
+    scale = 1.0 / math.sqrt(HD)
+
+    def slope_row(h, size):
+        index = jnp.full((1, size), col * heads + h + 1, i32).astype(f32)
+        return jnp.exp(index * (-8.0 / H * math.log(2.0)))
+
+    def attend(i):
+        g = group_at(i)
+        prefix_copy(g).wait()
+        tail_copy(g).wait()
+        cont = g * lax.div(rows, 2) + row_cont
+        prompt_of_row = lax.div(cont, CONT)
+        spots = lax.broadcasted_iota(i32, (rows, tail_row.shape[1]), 1)
+        own_tail = jnp.sum(
+            jnp.where(spots == cont, tail_row[...], 0.0), axis=1, keepdims=True
+        )
+        query_off = own_tail + step.astype(f32)
+
+        lane = lax.broadcasted_iota(i32, (1, pair_pages * tokens), 1)
+        slot = lax.div(lane, tokens)
+        token = lax.rem(lane, tokens) + row * tokens
+        owner = jnp.zeros_like(lane)
+        place = jnp.zeros_like(lane)
+        length = jnp.zeros_like(lane)
+        for k in range(pair_pages):
+            item = prefix_item[me * slots + g * pair_pages + k]
+            prompt = lax.div(item, MAXPAGES)
+            hit = slot == k
+            owner = jnp.where(hit, prompt, owner)
+            place = jnp.where(hit, (item - prompt * MAXPAGES) * PAGE, place)
+            length = jnp.where(hit, prefix_length[prompt], length)
+        place = place + token
+        gap = (place - length).astype(f32)
+        open_prompt = jnp.where(place < length, owner, -1)
+        prefix_gap = jnp.where(open_prompt == prompt_of_row, gap - query_off, masked_score)
+
+        lane = lax.broadcasted_iota(i32, (1, pair_tails * tokens), 1)
+        slot = lax.div(lane, tokens)
+        token = lax.rem(lane, tokens) + row * tokens
+        owner = jnp.zeros_like(lane)
+        length = jnp.zeros_like(lane)
+        for k in range(pair_tails):
+            item = tail_item[me * tails + g * pair_tails + k]
+            hit = slot == k
+            owner = jnp.where(hit, item, owner)
+            length = jnp.where(hit, tail_length[item], length)
+        gap = (token - length).astype(f32)
+        open_cont = jnp.where(token < length, owner, -1)
+        tail_gap = jnp.where(open_cont == cont, gap - step.astype(f32), masked_score)
+
+        pre = pl.ds(g * pair_pages, pair_pages)
+        tai = pl.ds(g * pair_tails, pair_tails)
+        levels = []
+        for h in range(heads):
+            hs = slice(h * HD, (h + 1) * HD)
+            query = q_buf[g, :, hs]
+            keys = prefix_v[pre, 0, :, hs].reshape(pair_pages * tokens, HD)
+            tail_keys = tail_v[tai, 0, :, hs].reshape(pair_tails * tokens, HD)
+            s_one = (
+                lax.dot_general(query, keys, contract_last, preferred_element_type=f32) * scale
+                + slope_row(h, pair_pages * tokens) * prefix_gap
+            )
+            s_two = (
+                lax.dot_general(query, tail_keys, contract_last, preferred_element_type=f32)
+                * scale
+                + slope_row(h, pair_tails * tokens) * tail_gap
+            )
+            top = jnp.maximum(
+                jnp.max(s_one, axis=1, keepdims=True), jnp.max(s_two, axis=1, keepdims=True)
+            )
+            top = jnp.maximum(top, empty_floor)
+            w_one = jnp.exp(s_one - top)
+            w_two = jnp.exp(s_two - top)
+            total = jnp.sum(w_one, axis=1, keepdims=True) + jnp.sum(w_two, axis=1, keepdims=True)
+            total = jnp.maximum(total, 1e-30)
+            values = prefix_v[pre, 1, :, hs].reshape(pair_pages * tokens, HD)
+            tail_values = tail_v[tai, 1, :, hs].reshape(pair_tails * tokens, HD)
+            out = jnp.dot(w_one.astype(bf16), values, preferred_element_type=f32) + jnp.dot(
+                w_two.astype(bf16), tail_values, preferred_element_type=f32
+            )
+            p_stage[g, :, hs] = (out / total).astype(bf16)
+            levels.append(top + jnp.log(total))
+        l_stage[g] = columns_to_tile(levels)
+
+    def partial_copies(i, k):
+        g = group_at(i)
+        target = (g, row_at(k), col)
+        return (
+            remote(
+                p_stage.at[g], p_buf.at[me, row], p_send.at[g, k], p_recv.at[me, row], target
+            ),
+            remote(
+                l_stage.at[g], l_buf.at[me, row], l_send.at[g, k], l_recv.at[me, row], target
+            ),
+        )
+
+    def partial_arrivals(i, k):
+        g, r = group_at(i), row_at(k)
+        return (
+            remote(p_stage.at[g], p_buf.at[g, r], p_send.at[g, k], p_recv.at[g, r], (g, r, col)),
+            remote(l_stage.at[g], l_buf.at[g, r], l_send.at[g, k], l_recv.at[g, r], (g, r, col)),
+        )
+
+    attend(jnp.int32(0))
+    for k in range(1, R):
+        for copy in partial_copies(jnp.int32(0), k):
+            copy.start()
+    p_buf[me, row] = p_stage[me]
+    l_buf[me, row] = l_stage[me]
+
+    def next_group(i, carry):
+        g = group_at(i)
+        remote(fresh.at[0], q_buf.at[g], q_send.at[i], q_recv.at[g], (g, row, col)).wait_recv()
+        attend(i)
+        for k in range(R):
+            for copy in partial_copies(i, k):
+                copy.start()
+        return carry
+
+    lax.fori_loop(1, G, next_group, 0)
+
+    key_id = lax.broadcasted_iota(i32, (rows, rows), 1)
+    new_ok = jnp.logical_and(lax.div(key_id, 2) == row_cont, lax.rem(key_id, 2) <= step)
+    new_gap = jnp.where(new_ok, (lax.rem(key_id, 2) - step).astype(f32), masked_score)
+    levels, new_outs = [], []
+    for h in range(heads):
+        hs = slice(h * HD, (h + 1) * HD)
+        scores = (
+            lax.dot_general(
+                fresh[0, :, hs], fresh[1, :, hs], contract_last, preferred_element_type=f32
+            )
+            * scale
+            + slope_row(h, rows) * new_gap
+        )
+        top = jnp.max(scores, axis=1, keepdims=True)
+        weights = jnp.exp(scores - top)
+        total = jnp.sum(weights, axis=1, keepdims=True)
+        new_outs.append(
+            jnp.dot(weights.astype(bf16), fresh[2, :, hs], preferred_element_type=f32) / total
+        )
+        levels.append(top + jnp.log(total))
+    new_level = columns_to_tile(levels)
+
+    for i in range(G):
+        for k in range(R):
+            if i or k:
+                for copy in partial_arrivals(jnp.int32(i), k):
+                    copy.wait_recv()
+
+    peers = [l_buf[g, r] for g in range(G) for r in range(R)] + [new_level]
+    peak = peers[0]
+    for level in peers[1:]:
+        peak = jnp.maximum(peak, level)
+    shares = [jnp.exp(level - peak) for level in peers]
+    total = shares[0]
+    for part in shares[1:]:
+        total = total + part
+    scaled = [part / total for part in shares]
+    groups_of_tiles = [
+        tile_to_columns(jnp.concatenate(scaled[at : at + LANES // STAT], axis=0), rows)
+        for at in range(0, len(scaled), LANES // STAT)
+    ]
+
+    def weight_of(peer, h):
+        block, spot = divmod(peer, LANES // STAT)
+        at = spot * STAT + h
+        return groups_of_tiles[block][:, at : at + 1]
+
+    for h in range(heads):
+        hs = slice(h * HD, (h + 1) * HD)
+        joined = weight_of(G * R, h) * new_outs[h]
+        for g in range(G):
+            for r in range(R):
+                joined = joined + weight_of(g * R + r, h) * p_buf[g, r, :, hs].astype(f32)
+        att[:, hs] = joined.astype(bf16)
+
+    def share_of(k):
+        return pl.ds(pl.multiple_of(col_at(k) * share, LANES), share)
+
+    weight_copies[0].wait()
+    for k in range(1, C):
+        t = col_at(k)
+        a_stage[k] = jnp.dot(
+            att[...], out_w[:, share_of(k)], preferred_element_type=f32
+        ).astype(bf16)
+        copy = remote(a_stage.at[k], a_buf.at[col], a_send.at[k], a_recv.at[col], (me, row, t))
+        copy.start()
+        sends.append(copy)
+    vec = {}
+    at = 0
+    for name, size in (
+        ("out_bias", share),
+        ("down_bias", share),
+        ("mlp_gain", width),
+        ("mlp_shift", width),
+        ("next_gain", width),
+        ("next_shift", width),
+        ("score_weight", width),
+        ("up_bias", chunks * chunk // R),
+        ("qkv_bias", pieces * piece),
+    ):
+        vec[name] = (at, size)
+        at += size
+
+    def vector(name, start=0, size=None):
+        base, full = vec[name]
+        return vectors[:, base + start : base + start + (full if size is None else size)]
+
+    total = (
+        jnp.dot(att[...], out_w[:, share_of(0)], preferred_element_type=f32)
+        + residual[...].astype(f32)
+        + vector("out_bias")
+    )
+    for k in range(1, C):
+        src = col_at(C - k)
+        remote(
+            a_stage.at[k], a_buf.at[src], a_send.at[k], a_recv.at[src], (me, row, src)
+        ).wait_recv()
+        total = total + a_buf[src].astype(f32)
+    hidden[...] = total
+
+    def gather(own, tile, wide_buf, wide_send, wide_recv, small_buf, small_send, small_recv):
+        small_buf[row, col] = tile
+        wide_buf[col] = own
+        for k in range(R):
+            for j in range(C):
+                if k or j:
+                    copy = remote(
+                        small_buf.at[row, col],
+                        small_buf.at[row, col],
+                        small_send.at[k, j],
+                        small_recv.at[row, col],
+                        (me, row_at(k), col_at(j)),
+                    )
+                    copy.start()
+                    sends.append(copy)
+        for j in range(1, C):
+            copy = remote(
+                wide_buf.at[col],
+                wide_buf.at[col],
+                wide_send.at[j],
+                wide_recv.at[col],
+                (me, row, col_at(j)),
+            )
+            copy.start()
+            sends.append(copy)
+        for k in range(R):
+            for j in range(C):
+                if k or j:
+                    r, c = row_at(k), col_at(j)
+                    remote(
+                        small_buf.at[row, col],
+                        small_buf.at[r, c],
+                        small_send.at[k, j],
+                        small_recv.at[r, c],
+                        (me, r, c),
+                    ).wait_recv()
+        sums = small_buf[0, 0]
+        for k in range(1, R * C):
+            sums = sums + small_buf[k // C, k % C]
+        for j in range(1, C):
+            c = col_at(j)
+            remote(
+                wide_buf.at[col], wide_buf.at[c], wide_send.at[j], wide_recv.at[c], (me, row, c)
+            ).wait_recv()
+        return sums
+
+    def norm_into(sums, wide_buf, gain, shift):
+        columns = tile_to_columns(sums, rows)
+        center = columns[:, 0:1] / D
+        spread = columns[:, 1:2] / D - center * center
+        factor = lax.rsqrt(spread + norm_eps)
+        for c in range(C):
+            normed[:, c * share : (c + 1) * share] = (
+                (wide_buf[c].astype(f32) - center) * factor * vector(gain, c * share, share)
+                + vector(shift, c * share, share)
+            ).astype(bf16)
+
+    sums = gather(
+        total.astype(bf16),
+        columns_to_tile(
+            [
+                jnp.sum(total, axis=1, keepdims=True),
+                jnp.sum(total * total, axis=1, keepdims=True),
+            ]
+        ),
+        x_buf,
+        x_send,
+        x_recv,
+        s_buf,
+        s_send,
+        s_recv,
+    )
+    norm_into(sums, x_buf, "mlp_gain", "mlp_shift")
+
+    partner = (me, row_at(1), col)
+    weight_copies[1].wait()
+    per_row = chunks // R
+    for n in range(chunks):
+        part = jnp.dot(
+            normed[...], up_w[:, n * chunk : (n + 1) * chunk], preferred_element_type=f32
+        )
+        mine = jnp.where(jnp.full((1, chunk), row, i32) == n // per_row, 1.0, 0.0)
+        part = part + mine * vector("up_bias", (n % per_row) * chunk, chunk)
+        u_own[n] = part
+        u_stage[n] = part.astype(bf16)
+        copy = remote(u_stage.at[n], u_buf.at[n], u_send.at[n], u_recv.at[n], partner)
+        copy.start()
+        sends.append(copy)
+
+    weight_copies[2].wait()
+    last = chunks - 1
+    for n in range(chunks):
+        remote(u_stage.at[n], u_buf.at[n], u_send.at[n], u_recv.at[n], partner).wait_recv()
+        v = u_own[n] + u_buf[n].astype(f32)
+        gelu = (0.5 * v * (1.0 + jnp.tanh(0.7978845608 * (v + 0.044715 * (v * v * v))))).astype(
+            bf16
+        )
+        if n < last:
+            term = jnp.dot(
+                gelu, down_w[n * chunk : (n + 1) * chunk, :], preferred_element_type=f32
+            )
+            acc[...] = term if n == 0 else acc[...] + term
+
+    def down_for(k):
+        return acc[:, share_of(k)] + jnp.dot(
+            gelu, down_w[last * chunk :, share_of(k)], preferred_element_type=f32
+        )
+
+    for k in range(1, C):
+        d_stage[k] = down_for(k).astype(bf16)
+        copy = remote(
+            d_stage.at[k], d_buf.at[col], d_send.at[k], d_recv.at[col], (me, row, col_at(k))
+        )
+        copy.start()
+        sends.append(copy)
+    total = down_for(0) + hidden[...] + vector("down_bias")
+    for k in range(1, C):
+        src = col_at(C - k)
+        remote(
+            d_stage.at[k], d_buf.at[src], d_send.at[k], d_recv.at[src], (me, row, src)
+        ).wait_recv()
+        total = total + d_buf[src].astype(f32)
+    layer_out = total.astype(bf16)
+    layer_ref[...] = layer_out
+    wide = layer_out.astype(f32)
+    base = vec["score_weight"][0]
+    score_part = vectors[:, pl.ds(pl.multiple_of(base + col * share, LANES), share)]
+    sums = gather(
+        layer_out,
+        columns_to_tile(
+            [
+                jnp.sum(wide, axis=1, keepdims=True),
+                jnp.sum(wide * wide, axis=1, keepdims=True),
+                jnp.sum(wide * score_part, axis=1, keepdims=True),
+            ]
+        ),
+        y_buf,
+        y_send,
+        y_recv,
+        t_buf,
+        t_send,
+        t_recv,
+    )
+    stat_ref[...] = sums
+    norm_into(sums, y_buf, "next_gain", "next_shift")
+
+    weight_copies[3].wait()
+    half = pieces * piece
+
+    def qkv_piece(r, n):
+        at = pl.ds(pl.multiple_of(r * half + n * piece, LANES), piece)
+        return jnp.dot(normed[...], qkv_w[:, at], preferred_element_type=f32)
+
+    for n in range(pieces):
+        z_stage[n] = qkv_piece(row_at(1), n).astype(bf16)
+        copy = remote(z_stage.at[n], z_buf.at[n], z_send.at[n], z_recv.at[n], partner)
+        copy.start()
+        sends.append(copy)
+    for n in range(pieces):
+        own = qkv_piece(row, n) + vector("qkv_bias", n * piece, piece)
+        remote(z_stage.at[n], z_buf.at[n], z_send.at[n], z_recv.at[n], partner).wait_recv()
+        proj_ref[:, n * piece : (n + 1) * piece] = (own + z_buf[n].astype(f32)).astype(bf16)
+
+    for copy in sends:
+        copy.wait_send()
+    for i in range(G):
+        for k in range(R):
+            if i or k:
+                for copy in partial_copies(jnp.int32(i), k):
+                    copy.wait_send()
+
+
+def fused_shards(
+    sizes,
+    residual,
+    fresh_qkv,
+    prefix_pages,
+    tail_pages,
+    prefix_item,
+    tail_item,
+    prefix_length,
+    tail_length,
+    out_weight,
+    out_bias,
+    mlp_gain,
+    mlp_shift,
+    up_weight,
+    up_bias,
+    down_weight,
+    down_bias,
+    next_gain,
+    next_shift,
+    score_weight,
+    qkv_weight,
+    qkv_bias,
+):
+    G, R, C = sizes["pages"], sizes["row"], sizes["col"]
+    f32, bf16 = jnp.float32, jnp.bfloat16
+    cont_local, _, share = residual.shape
+    rows = cont_local * 2
+    head_width = fresh_qkv.shape[3]
+    ff_local = up_weight.shape[1]
+    out_local = qkv_bias.shape[0]
+    chunk = ff_local // 4
+    piece = out_local // 2
+    vectors = jnp.concatenate(
+        [
+            out_bias,
+            down_bias,
+            mlp_gain,
+            mlp_shift,
+            next_gain,
+            next_shift,
+            score_weight,
+            up_bias,
+            qkv_bias,
+        ]
+    ).astype(f32)[None, :]
+    fresh = fresh_qkv.reshape(rows, 3, head_width).transpose(1, 0, 2)
+    vmem = pl.BlockSpec(memory_space=pltpu.VMEM)
+    smem = pl.BlockSpec(memory_space=pltpu.SMEM)
+    anywhere = pl.BlockSpec(memory_space=pl.ANY)
+    dma = pltpu.SemaphoreType.DMA
+    layer_out, stats, projected = pl.pallas_call(
+        lambda *refs: layer_kernel(sizes, *refs),
+        out_shape=(
+            jax.ShapeDtypeStruct((rows, share), bf16),
+            jax.ShapeDtypeStruct((STAT, LANES), f32),
+            jax.ShapeDtypeStruct((rows, out_local), bf16),
+        ),
+        in_specs=[smem] * 4 + [vmem] * 4 + [anywhere] * 6,
+        out_specs=(vmem, vmem, vmem),
+        scratch_shapes=[
+            pltpu.VMEM(prefix_pages.shape, bf16),
+            pltpu.VMEM(tail_pages.shape, bf16),
+            pltpu.VMEM(out_weight.shape, bf16),
+            pltpu.VMEM(up_weight.shape, bf16),
+            pltpu.VMEM(down_weight.shape, bf16),
+            pltpu.VMEM(qkv_weight.shape, bf16),
+            pltpu.VMEM((G, rows, head_width), bf16),
+            pltpu.VMEM((G, rows, head_width), bf16),
+            pltpu.VMEM((G, STAT, LANES), f32),
+            pltpu.VMEM((G, R, rows, head_width), bf16),
+            pltpu.VMEM((G, R, STAT, LANES), f32),
+            pltpu.VMEM((rows, head_width), bf16),
+            pltpu.VMEM((C, rows, share), bf16),
+            pltpu.VMEM((C, rows, share), bf16),
+            pltpu.VMEM((rows, share), f32),
+            pltpu.VMEM((C, rows, share), bf16),
+            pltpu.VMEM((R, C, STAT, LANES), f32),
+            pltpu.VMEM((rows, C * share), bf16),
+            pltpu.VMEM((ff_local // chunk, rows, chunk), f32),
+            pltpu.VMEM((ff_local // chunk, rows, chunk), bf16),
+            pltpu.VMEM((ff_local // chunk, rows, chunk), bf16),
+            pltpu.VMEM((rows, C * share), f32),
+            pltpu.VMEM((C, rows, share), bf16),
+            pltpu.VMEM((C, rows, share), bf16),
+            pltpu.VMEM((C, rows, share), bf16),
+            pltpu.VMEM((R, C, STAT, LANES), f32),
+            pltpu.VMEM((out_local // piece, rows, piece), bf16),
+            pltpu.VMEM((out_local // piece, rows, piece), bf16),
+            dma((G, 2)),
+            dma((4,)),
+            dma((G,)),
+            dma((G,)),
+            dma((G, R)),
+            dma((G, R)),
+            dma((G, R)),
+            dma((G, R)),
+            dma((C,)),
+            dma((C,)),
+            dma((C,)),
+            dma((C,)),
+            dma((R, C)),
+            dma((R, C)),
+            dma((ff_local // chunk,)),
+            dma((ff_local // chunk,)),
+            dma((C,)),
+            dma((C,)),
+            dma((C,)),
+            dma((C,)),
+            dma((R, C)),
+            dma((R, C)),
+            dma((out_local // piece,)),
+            dma((out_local // piece,)),
+        ],
+        compiler_params=pltpu.CompilerParams(
+            collective_id=0, has_side_effects=True, vmem_limit_bytes=48 * 1024 * 1024
+        ),
+        name="fused_layer",
+    )(
+        prefix_item,
+        tail_item,
+        prefix_length,
+        tail_length,
+        tail_length.astype(f32)[None, :],
+        fresh,
+        residual.reshape(rows, share),
+        vectors,
+        prefix_pages,
+        tail_pages,
+        out_weight,
+        up_weight,
+        down_weight,
+        qkv_weight,
+    )
+    return (
+        layer_out.reshape(cont_local, 2, share),
+        stats[2, :rows].reshape(cont_local, 2),
+        projected.reshape(cont_local, 2, out_local),
+    )
+
+
+def shards(residual, fresh_qkv, prefix_pages, *others):
+    sizes = {axis: lax.axis_size(axis) for axis in ("pages", "row", "col")}
+    share, tokens = residual.shape[2], prefix_pages.shape[2]
+    if sizes["row"] == 2 and sizes["pages"] % 2 == 0 and share % LANES == 0 and tokens % 16 == 0:
+        return fused_shards(sizes, residual, fresh_qkv, prefix_pages, *others)
+    return plain_shards(residual, fresh_qkv, prefix_pages, *others)
+
+
 def solution(mesh):
     in_specs = (
         P("pages", None, ("row", "col")),

time: 304 us -> 68.6 us (0.23)
  blocking collectives: 107 us -> 0 us
  waiting for transfers between devices: 60.1 us -> 0 us
  Pallas kernels: 0 us -> 51.1 us
  local copies, waits for them, and re-layouts: 56.5 us -> 15.6 us
  matrix products: 26.4 us -> 0 us
  other arithmetic: 26.2 us -> 0.69 us
  between operations: 14.4 us -> 0.67 us
  starting transfers between devices: 11.5 us -> 0 us
    reduce_scatter x4 -> x0, waiting for transfers between devices: 58.2 us -> none  [the longest x1 20.6 us: shards(): lax.psum_scatter(head_term, 'col', scatter_dimension=1, tiled=True)]
    all_gather x7 -> x0, blocking collectives: 54.2 us -> none  [the longest x3 14.3 us: combined_all(): everything = jax.tree.map(lambda part: lax.all_gather(part, axis), shard)]
    psum x2 -> x0, blocking collectives: 53.2 us -> none  [the longest x1 34.5 us: shards(): lax.psum((jnp.sum(out_wide, axis=1), jnp.sum(out_wide * out_wide, axis=1)...]
    pallas_call x0 -> x1, Pallas kernels: none -> 51.1 us  [fused_shards(): pl.pallas_call(lambda *refs: layer_kernel(sizes, *refs), out_shape=(jax.S...]
    dot_general x10 -> x0, matrix products: 26.4 us -> none  [the longest x3 9.31 us: slot_partials(): jnp.einsum('sqhk,skhd->sqhd', weights, page_values.astype(jnp.float32), p...]
    another operation x7 -> x1, local copies, waits for them, and re-layouts: 15 us -> 0.1 us  [fused_shards(): stats[2, :rows].reshape(cont_local, 2)]
    all_to_all x3 -> x0, starting transfers between devices: 11.4 us -> none  [the longest x1 4.14 us: shards(): lax.all_to_all(outputs.reshape(group_count, row_total, head_count, HD), '...]
    slice x8 -> x1, local copies, waits for them, and re-layouts: 9.81 us -> 0.02 us  [fused_shards(): stats[2, :rows].reshape(cont_local, 2)]
  transfers between devices with their start and end apart: 7 -> 0, of which waited for: 5 -> 0; matrix products, arithmetic and copies ran while one was open for 14% -> 0% of each run, Pallas kernels for 0% -> 0%
where the time goes in v1:
time: 68.6 us; the launch traced here: 68 us
  Pallas kernels  51.1 us (74%)
  local copies, waits for them, and re-layouts  15.6 us (23%)
  other arithmetic  0.69 us (1%)
    pallas_call x1, Pallas kernels, fused_shards(): pl.pallas_call(lambda *refs: layer_kernel(sizes, *refs), out_shape=(jax.S...  51.1 us
    unnamed x22, local copies, waits for them, and re-layouts  12.6 us

profile of v1, /device:TPU:0, one launch (start us, length us, event | category | flops | bytes accessed | tf_op | source)
XLA Modules:
  0.0 68.0 jit_solution(14263607410601178411)
XLA Ops:
  0.6 1.1 %copy.26 = bf16[32,2,3,512]{3,1,0,2:T(2,128)(2,1)S(1)} copy(bf16[32,2,3,512]{3,1,2,0:T(2,128)(2,1)} %param.22) | data formatting | bytes 393216 | tf_op args[1]
  1.7 0.1 reshape.138
  1.8 0.7 constant_dynamic-update-slice_fusion.8
  2.4 0.7 constant_dynamic-update-slice_fusion.7
  3.1 0.7 %constant_dynamic-update-slice_fusion.6 = bf16[1,7424]{1,0:T(2,128)(2,1)S(1)} fusion(bf16[1,7424]{1,0:T(2,128)(2,1)S(1)} %constant_dynamic-update-slice_fusion.7, bf16[1024]{0:T(1024)(128)(2,1)} %param.31), kind=kLoop, calls=%fused_computation.6 | loop fusion | bytes 6144
  3.8 0.7 %constant_dynamic-update-slice_fusion.5 = bf16[1,7424]{1,0:T(2,128)(2,1)S(1)} fusion(bf16[1,7424]{1,0:T(2,128)(2,1)S(1)} %constant_dynamic-update-slice_fusion.6, bf16[1024]{0:T(1024)(128)(2,1)} %param.32), kind=kLoop, calls=%fused_computation.5 | loop fusion | bytes 6144
  4.5 0.7 %constant_dynamic-update-slice_fusion.4 = bf16[1,7424]{1,0:T(2,128)(2,1)S(1)} fusion(bf16[1,7424]{1,0:T(2,128)(2,1)S(1)} %constant_dynamic-update-slice_fusion.5, bf16[1024]{0:T(1024)(128)(2,1)} %param.37), kind=kLoop, calls=%fused_computation.4 | loop fusion | bytes 6144
  5.2 0.7 %constant_dynamic-update-slice_fusion.3 = bf16[1,7424]{1,0:T(2,128)(2,1)S(1)} fusion(bf16[1,7424]{1,0:T(2,128)(2,1)S(1)} %constant_dynamic-update-slice_fusion.4, bf16[1024]{0:T(1024)(128)(2,1)} %param.38), kind=kLoop, calls=%fused_computation.3 | loop fusion | bytes 6144
  5.9 0.7 %constant_dynamic-update-slice_fusion.2 = bf16[1,7424]{1,0:T(2,128)(2,1)S(1)} fusion(bf16[1,7424]{1,0:T(2,128)(2,1)S(1)} %constant_dynamic-update-slice_fusion.3, bf16[1024]{0:T(1024)(128)(2,1)} %param.39), kind=kLoop, calls=%fused_computation.2 | loop fusion | bytes 6144
  6.6 0.7 %constant_dynamic-update-slice_fusion.1 = bf16[1,7424]{1,0:T(2,128)(2,1)S(1)} fusion(bf16[1,7424]{1,0:T(2,128)(2,1)S(1)} %constant_dynamic-update-slice_fusion.2, bf16[1024]{0:T(1024)(128)(2,1)} %param.34), kind=kLoop, calls=%fused_computation.1 | loop fusion | bytes 6144
  7.3 0.7 %constant_dynamic-update-slice_fusion = bf16[1,7424]{1,0:T(2,128)(2,1)S(1)} fusion(bf16[1,7424]{1,0:T(2,128)(2,1)S(1)} %constant_dynamic-update-slice_fusion.1, bf16[768]{0:T(1024)(128)(2,1)} %param.41), kind=kLoop, calls=%fused_computation | loop fusion | bytes 4608 | tf_op jit(solution)/shard_map/concatenate | solution.py:948
  8.0 0.8 %reshape.139.refs_6_ = bf16[64,256]{1,0:T(8,128)(2,1)S(1)} reshape(bf16[32,2,256]{2,1,0:T(2,128)(2,1)} %param.21) | data formatting | bytes 65536 | tf_op jit(solution)/shard_map/reshape | solution.py:1040
  8.8 0.7 convert_bitcast_fusion.refs_4_
  9.4 0.0 copy-start
  9.4 1.6 %copy-done = bf16[16,2,64,512]{3,2,1,0:T(8,128)(2,1)S(1)} copy-done((bf16[16,2,64,512]{3,2,1,0:T(8,128)(2,1)S(1)}, bf16[16,2,64,512]{3,2,1,0:T(8,128)(2,1)}, u32[]{:S(2)}) %copy-start) | copy-done | bytes 2097176
  11.0 0.0 copy-start.1
  11.0 1.2 %copy-done.1 = bf16[512,1024]{1,0:T(8,128)(2,1)S(1)} copy-done((bf16[512,1024]{1,0:T(8,128)(2,1)S(1)}, bf16[512,1024]{1,0:T(8,128)(2,1)}, u32[]{:S(2)}) %copy-start.1) | copy-done | bytes 1048600
  12.2 0.0 copy-start.2
  12.2 0.7 copy-done.2
  12.9 0.0 copy-start.3
  12.9 0.7 copy-done.3
  13.6 0.0 copy-start.4
  13.6 0.7 copy-done.4
  14.2 0.0 copy-start.5
  14.2 0.7 copy-done.5
  14.9 51.1 %fused_layer.1 = (bf16[64,256]{1,0:T(8,128)(2,1)S(1)}, f32[8,128]{1,0:T(8,128)S(1)}, bf16[64,768]{1,0:T(8,128)(2,1)S(1)}) custom-call(s32[64]{0:T(128)S(1)} %copy-done.2, s32[128]{0:T(128)S(1)} %copy-done.3, s32[8]{0:T(128)S(1)} %copy-done.4, s32[128]{0:T(128)S(1)} %copy-done.5, f32[1,128]{1,0:T(1,128)S(1)} %convert_bitcast_fusion.refs_4_, ...), custom_call_target="tpu_custom_call" | custom-call | tf_op jit(solution)/shard_map/fused_layer/pallas_call | solution.py:966
  66.0 0.7 %reshape.141 = bf16[32,2,768]{2,1,0:T(2,128)(2,1)} reshape(bf16[64,768]{1,0:T(8,128)(2,1)S(1)} %get-tuple-element.8) | data formatting | bytes 196608 | tf_op jit(solution)/shard_map/reshape | solution.py:1052
  66.6 0.6 reshape.140
  67.3 0.1 reshape_squeeze.3
  67.4 0.6 copy.27
  (2 shorter events, 0.1 us)
Async XLA Ops:
  9.4 1.6 %copy-start = (bf16[16,2,64,512]{3,2,1,0:T(8,128)(2,1)S(1)}, bf16[16,2,64,512]{3,2,1,0:T(8,128)(2,1)}, u32[]{:S(2)}) copy-start(bf16[16,2,64,512]{3,2,1,0:T(8,128)(2,1)} %refs_8_.1) | copy-start | bytes 6291460
  11.0 1.2 %copy-start.1 = (bf16[512,1024]{1,0:T(8,128)(2,1)S(1)}, bf16[512,1024]{1,0:T(8,128)(2,1)}, u32[]{:S(2)}) copy-start(bf16[512,1024]{1,0:T(8,128)(2,1)} %refs_10_.1) | copy-start | bytes 3145732
  12.2 0.7 copy-start.2
  12.9 0.7 copy-start.3
  13.6 0.7 copy-start.4
  14.2 0.7 copy-start.5

commit v2 on v1

--- a/solution.py
+++ b/solution.py
@@ -354,14 +354,21 @@
 
 def layer_kernel(
     sizes,
-    prefix_item,
-    tail_item,
-    prefix_length,
-    tail_length,
-    tail_row,
-    fresh,
-    residual,
-    vectors,
+    item_hbm,
+    owner_hbm,
+    length_hbm,
+    span_hbm,
+    fresh_hbm,
+    residual_hbm,
+    out_bias_hbm,
+    mlp_gain_hbm,
+    mlp_shift_hbm,
+    up_bias_hbm,
+    down_bias_hbm,
+    next_gain_hbm,
+    next_shift_hbm,
+    score_hbm,
+    qkv_bias_hbm,
     prefix_hbm,
     tail_hbm,
     out_hbm,
@@ -371,6 +378,25 @@
     layer_ref,
     stat_ref,
     proj_ref,
+    prefix_item,
+    tail_item,
+    prefix_length,
+    tail_length,
+    tail_row,
+    fresh_raw,
+    residual,
+    out_bias,
+    mlp_gain,
+    mlp_shift,
+    up_bias,
+    down_bias,
+    next_gain,
+    next_shift,
+    score_weight,
+    qkv_bias,
+    fresh,
+    new_out,
+    small_sem,
     prefix_v,
     tail_v,
     out_w,
@@ -429,8 +455,8 @@
     me = lax.axis_index("pages")
     row = lax.axis_index("row")
     col = lax.axis_index("col")
-    rows = residual.shape[0]
-    share = residual.shape[1]
+    rows = fresh.shape[1]
+    share = residual.shape[2]
     width = C * share
     heads = fresh.shape[2] // HD
     slots, _, tokens, _ = prefix_v.shape
@@ -440,7 +466,10 @@
     pieces, _, piece = z_buf.shape
 
     def group_at(i):
-        return lax.rem(lax.div(me, 2) + lax.div(i, 2), G // 2) * 2 + lax.rem(me + i, 2)
+        if isinstance(i, int) and i == 0:
+            return me
+        j = lax.rem(jnp.int32(i), G - 1) + 1
+        return lax.rem(lax.div(me, 2) + lax.div(j, 2), G // 2) * 2 + lax.rem(me + j, 2)
 
     def row_at(k):
         return lax.rem(row + k, R)
@@ -473,9 +502,28 @@
         )
     ]
 
-    for i in range(G):
-        prefix_copy(group_at(jnp.int32(i))).start()
-        tail_copy(group_at(jnp.int32(i))).start()
+    small_pairs = (
+        (fresh_hbm, fresh_raw),
+        (item_hbm, prefix_item),
+        (owner_hbm, tail_item),
+        (length_hbm, prefix_length),
+        (span_hbm, tail_length),
+        (span_hbm, tail_row),
+        (residual_hbm, residual),
+        (out_bias_hbm, out_bias),
+        (mlp_gain_hbm, mlp_gain),
+        (mlp_shift_hbm, mlp_shift),
+        (up_bias_hbm, up_bias),
+        (down_bias_hbm, down_bias),
+        (next_gain_hbm, next_gain),
+        (next_shift_hbm, next_shift),
+        (score_hbm, score_weight),
+        (qkv_bias_hbm, qkv_bias),
+    )
+    small_copies = [
+        pltpu.make_async_copy(src, dst, small_sem.at[k])
+        for k, (src, dst) in enumerate(small_pairs)
+    ]
 
     barrier = pltpu.get_barrier_semaphore()
     met = 0
@@ -486,7 +534,7 @@
                 pl.semaphore_signal(
                     barrier,
                     inc=1,
-                    device_id=(group_at(jnp.int32(i)), row_at(k), col),
+                    device_id=(group_at(i), row_at(k), col),
                     device_id_type=pl.DeviceIdType.MESH,
                 )
     for k in range(R):
@@ -498,6 +546,50 @@
                 device_id=(me, row_at(k), col_at(j)),
                 device_id_type=pl.DeviceIdType.MESH,
             )
+    for copy in small_copies[:6]:
+        copy.start()
+    for i in range(G):
+        prefix_copy(group_at(i)).start()
+        tail_copy(group_at(i)).start()
+    for copy in small_copies[6:]:
+        copy.start()
+
+    row_id = lax.broadcasted_iota(i32, (rows, 1), 0)
+    step = lax.rem(row_id, 2)
+    row_cont = lax.div(row_id, 2)
+    contract_last = (((1,), (1,)), ((), ()))
+    scale = 1.0 / math.sqrt(HD)
+
+    def slope_row(h, size):
+        index = jnp.full((1, size), col * heads + h + 1, i32).astype(f32)
+        return jnp.exp(index * (-8.0 / H * math.log(2.0)))
+
+    small_copies[0].wait()
+    for part in range(3):
+        fresh[part] = fresh_raw[:, part].reshape(rows, heads * HD)
+    q_buf[me] = fresh[0]
+    key_id = lax.broadcasted_iota(i32, (rows, rows), 1)
+    new_ok = jnp.logical_and(lax.div(key_id, 2) == row_cont, lax.rem(key_id, 2) <= step)
+    new_gap = jnp.where(new_ok, (lax.rem(key_id, 2) - step).astype(f32), masked_score)
+    levels = []
+    for h in range(heads):
+        hs = slice(h * HD, (h + 1) * HD)
+        scores = (
+            lax.dot_general(
+                fresh[0, :, hs], fresh[1, :, hs], contract_last, preferred_element_type=f32
+            )
+            * scale
+            + slope_row(h, rows) * new_gap
+        )
+        top = jnp.max(scores, axis=1, keepdims=True)
+        weights = jnp.exp(scores - top)
+        total = jnp.sum(weights, axis=1, keepdims=True)
+        new_out[:, hs] = (
+            jnp.dot(weights.astype(bf16), fresh[2, :, hs], preferred_element_type=f32) / total
+        )
+        levels.append(top + jnp.log(total))
+    new_level = columns_to_tile(levels)
+
     pl.semaphore_wait(barrier, met)
 
     sends = []
@@ -507,23 +599,14 @@
             q_buf.at[me],
             q_send.at[i],
             q_recv.at[me],
-            (group_at(jnp.int32(i)), row, col),
+            (group_at(i), row, col),
         )
         copy.start()
         sends.append(copy)
-    q_buf[me] = fresh[0]
     for copy in weight_copies:
         copy.start()
-
-    row_id = lax.broadcasted_iota(i32, (rows, 1), 0)
-    step = lax.rem(row_id, 2)
-    row_cont = lax.div(row_id, 2)
-    contract_last = (((1,), (1,)), ((), ()))
-    scale = 1.0 / math.sqrt(HD)
-
-    def slope_row(h, size):
-        index = jnp.full((1, size), col * heads + h + 1, i32).astype(f32)
-        return jnp.exp(index * (-8.0 / H * math.log(2.0)))
+    for copy in small_copies[1:]:
+        copy.wait()
 
     def attend(i):
         g = group_at(i)
@@ -531,9 +614,10 @@
         tail_copy(g).wait()
         cont = g * lax.div(rows, 2) + row_cont
         prompt_of_row = lax.div(cont, CONT)
-        spots = lax.broadcasted_iota(i32, (rows, tail_row.shape[1]), 1)
+        spots = lax.broadcasted_iota(i32, (rows, tail_row.shape[0]), 1)
+        tail_spans = tail_row[...].reshape(1, tail_row.shape[0]).astype(f32)
         own_tail = jnp.sum(
-            jnp.where(spots == cont, tail_row[...], 0.0), axis=1, keepdims=True
+            jnp.where(spots == cont, tail_spans, 0.0), axis=1, keepdims=True
         )
         query_off = own_tail + step.astype(f32)
 
@@ -622,9 +706,9 @@
             remote(l_stage.at[g], l_buf.at[g, r], l_send.at[g, k], l_recv.at[g, r], (g, r, col)),
         )
 
-    attend(jnp.int32(0))
+    attend(0)
     for k in range(1, R):
-        for copy in partial_copies(jnp.int32(0), k):
+        for copy in partial_copies(0, k):
             copy.start()
     p_buf[me, row] = p_stage[me]
     l_buf[me, row] = l_stage[me]
@@ -640,32 +724,10 @@
 
     lax.fori_loop(1, G, next_group, 0)
 
-    key_id = lax.broadcasted_iota(i32, (rows, rows), 1)
-    new_ok = jnp.logical_and(lax.div(key_id, 2) == row_cont, lax.rem(key_id, 2) <= step)
-    new_gap = jnp.where(new_ok, (lax.rem(key_id, 2) - step).astype(f32), masked_score)
-    levels, new_outs = [], []
-    for h in range(heads):
-        hs = slice(h * HD, (h + 1) * HD)
-        scores = (
-            lax.dot_general(
-                fresh[0, :, hs], fresh[1, :, hs], contract_last, preferred_element_type=f32
-            )
-            * scale
-            + slope_row(h, rows) * new_gap
-        )
-        top = jnp.max(scores, axis=1, keepdims=True)
-        weights = jnp.exp(scores - top)
-        total = jnp.sum(weights, axis=1, keepdims=True)
-        new_outs.append(
-            jnp.dot(weights.astype(bf16), fresh[2, :, hs], preferred_element_type=f32) / total
-        )
-        levels.append(top + jnp.log(total))
-    new_level = columns_to_tile(levels)
-
     for i in range(G):
         for k in range(R):
             if i or k:
-                for copy in partial_arrivals(jnp.int32(i), k):
+                for copy in partial_arrivals(i, k):
                     copy.wait_recv()
 
     peers = [l_buf[g, r] for g in range(G) for r in range(R)] + [new_level]
@@ -689,7 +751,7 @@
 
     for h in range(heads):
         hs = slice(h * HD, (h + 1) * HD)
-        joined = weight_of(G * R, h) * new_outs[h]
+        joined = weight_of(G * R, h) * new_out[:, hs]
         for g in range(G):
             for r in range(R):
                 joined = joined + weight_of(g * R + r, h) * p_buf[g, r, :, hs].astype(f32)
@@ -707,30 +769,14 @@
         copy = remote(a_stage.at[k], a_buf.at[col], a_send.at[k], a_recv.at[col], (me, row, t))
         copy.start()
         sends.append(copy)
-    vec = {}
-    at = 0
-    for name, size in (
-        ("out_bias", share),
-        ("down_bias", share),
-        ("mlp_gain", width),
-        ("mlp_shift", width),
-        ("next_gain", width),
-        ("next_shift", width),
-        ("score_weight", width),
-        ("up_bias", chunks * chunk // R),
-        ("qkv_bias", pieces * piece),
-    ):
-        vec[name] = (at, size)
-        at += size
-
-    def vector(name, start=0, size=None):
-        base, full = vec[name]
-        return vectors[:, base + start : base + start + (full if size is None else size)]
+
+    def vector(ref):
+        return ref[...].astype(f32).reshape(1, ref.shape[0])
 
     total = (
         jnp.dot(att[...], out_w[:, share_of(0)], preferred_element_type=f32)
-        + residual[...].astype(f32)
-        + vector("out_bias")
+        + residual[...].astype(f32).reshape(rows, share)
+        + vector(out_bias)
     )
     for k in range(1, C):
         src = col_at(C - k)
@@ -791,10 +837,11 @@
         center = columns[:, 0:1] / D
         spread = columns[:, 1:2] / D - center * center
         factor = lax.rsqrt(spread + norm_eps)
+        gains, shifts = vector(gain), vector(shift)
         for c in range(C):
-            normed[:, c * share : (c + 1) * share] = (
-                (wide_buf[c].astype(f32) - center) * factor * vector(gain, c * share, share)
-                + vector(shift, c * share, share)
+            at = slice(c * share, (c + 1) * share)
+            normed[:, at] = (
+                (wide_buf[c].astype(f32) - center) * factor * gains[:, at] + shifts[:, at]
             ).astype(bf16)
 
     sums = gather(
@@ -812,17 +859,18 @@
         s_send,
         s_recv,
     )
-    norm_into(sums, x_buf, "mlp_gain", "mlp_shift")
+    norm_into(sums, x_buf, mlp_gain, mlp_shift)
 
     partner = (me, row_at(1), col)
     weight_copies[1].wait()
     per_row = chunks // R
+    up_shift = vector(up_bias)
     for n in range(chunks):
         part = jnp.dot(
             normed[...], up_w[:, n * chunk : (n + 1) * chunk], preferred_element_type=f32
         )
         mine = jnp.where(jnp.full((1, chunk), row, i32) == n // per_row, 1.0, 0.0)
-        part = part + mine * vector("up_bias", (n % per_row) * chunk, chunk)
+        part = part + mine * up_shift[:, (n % per_row) * chunk : (n % per_row + 1) * chunk]
         u_own[n] = part
         u_stage[n] = part.astype(bf16)
         copy = remote(u_stage.at[n], u_buf.at[n], u_send.at[n], u_recv.at[n], partner)
@@ -855,7 +903,7 @@
         )
         copy.start()
         sends.append(copy)
-    total = down_for(0) + hidden[...] + vector("down_bias")
+    total = down_for(0) + hidden[...] + vector(down_bias)
     for k in range(1, C):
         src = col_at(C - k)
         remote(
@@ -865,8 +913,12 @@
     layer_out = total.astype(bf16)
     layer_ref[...] = layer_out
     wide = layer_out.astype(f32)
-    base = vec["score_weight"][0]
-    score_part = vectors[:, pl.ds(pl.multiple_of(base + col * share, LANES), share)]
+    scores = vector(score_weight)
+    score_part = scores[:, :share]
+    for c in range(1, C):
+        score_part = jnp.where(
+            jnp.full((1, share), col, i32) == c, scores[:, c * share : (c + 1) * share], score_part
+        )
     sums = gather(
         layer_out,
         columns_to_tile(
@@ -884,10 +936,11 @@
         t_recv,
     )
     stat_ref[...] = sums
-    norm_into(sums, y_buf, "next_gain", "next_shift")
+    norm_into(sums, y_buf, next_gain, next_shift)
 
     weight_copies[3].wait()
     half = pieces * piece
+    qkv_shift = vector(qkv_bias)
 
     def qkv_piece(r, n):
         at = pl.ds(pl.multiple_of(r * half + n * piece, LANES), piece)
@@ -899,7 +952,7 @@
         copy.start()
         sends.append(copy)
     for n in range(pieces):
-        own = qkv_piece(row, n) + vector("qkv_bias", n * piece, piece)
+        own = qkv_piece(row, n) + qkv_shift[:, n * piece : (n + 1) * piece]
         remote(z_stage.at[n], z_buf.at[n], z_send.at[n], z_recv.at[n], partner).wait_recv()
         proj_ref[:, n * piece : (n + 1) * piece] = (own + z_buf[n].astype(f32)).astype(bf16)
 
@@ -908,7 +961,7 @@
     for i in range(G):
         for k in range(R):
             if i or k:
-                for copy in partial_copies(jnp.int32(i), k):
+                for copy in partial_copies(i, k):
                     copy.wait_send()
 
 
@@ -945,23 +998,11 @@
     out_local = qkv_bias.shape[0]
     chunk = ff_local // 4
     piece = out_local // 2
-    vectors = jnp.concatenate(
-        [
-            out_bias,
-            down_bias,
-            mlp_gain,
-            mlp_shift,
-            next_gain,
-            next_shift,
-            score_weight,
-            up_bias,
-            qkv_bias,
-        ]
-    ).astype(f32)[None, :]
-    fresh = fresh_qkv.reshape(rows, 3, head_width).transpose(1, 0, 2)
+    fresh = fresh_qkv.transpose(0, 2, 1, 3)
+    one_row = (out_bias, mlp_gain, mlp_shift, up_bias, down_bias)
+    one_row = one_row + (next_gain, next_shift, score_weight, qkv_bias)
     vmem = pl.BlockSpec(memory_space=pltpu.VMEM)
-    smem = pl.BlockSpec(memory_space=pltpu.SMEM)
-    anywhere = pl.BlockSpec(memory_space=pl.ANY)
+    hbm = pl.BlockSpec(memory_space=pltpu.MemorySpace.HBM)
     dma = pltpu.SemaphoreType.DMA
     layer_out, stats, projected = pl.pallas_call(
         lambda *refs: layer_kernel(sizes, *refs),
@@ -970,9 +1011,20 @@
             jax.ShapeDtypeStruct((STAT, LANES), f32),
             jax.ShapeDtypeStruct((rows, out_local), bf16),
         ),
-        in_specs=[smem] * 4 + [vmem] * 4 + [anywhere] * 6,
+        in_specs=[hbm] * (12 + len(one_row)),
         out_specs=(vmem, vmem, vmem),
         scratch_shapes=[
+            pltpu.SMEM(prefix_item.shape, jnp.int32),
+            pltpu.SMEM(tail_item.shape, jnp.int32),
+            pltpu.SMEM(prefix_length.shape, jnp.int32),
+            pltpu.SMEM(tail_length.shape, jnp.int32),
+            pltpu.VMEM(tail_length.shape, jnp.int32),
+            pltpu.VMEM(fresh.shape, bf16),
+            pltpu.VMEM(residual.shape, bf16),
+            *(pltpu.VMEM(v.shape, bf16) for v in one_row),
+            pltpu.VMEM((3, rows, head_width), bf16),
+            pltpu.VMEM((rows, head_width), f32),
+            dma((7 + len(one_row),)),
             pltpu.VMEM(prefix_pages.shape, bf16),
             pltpu.VMEM(tail_pages.shape, bf16),
             pltpu.VMEM(out_weight.shape, bf16),
@@ -1027,7 +1079,7 @@
             dma((out_local // piece,)),
         ],
         compiler_params=pltpu.CompilerParams(
-            collective_id=0, has_side_effects=True, vmem_limit_bytes=48 * 1024 * 1024
+            collective_id=0, has_side_effects=True, vmem_limit_bytes=64 * 1024 * 1024
         ),
         name="fused_layer",
     )(
@@ -1035,10 +1087,9 @@
         tail_item,
         prefix_length,
         tail_length,
-        tail_length.astype(f32)[None, :],
         fresh,
-        residual.reshape(rows, share),
-        vectors,
+        residual,
+        *one_row,
         prefix_pages,
         tail_pages,
         out_weight,

time: 68.6 us -> 56.3 us (0.82)
  local copies, waits for them, and re-layouts: 15.6 us -> 4.39 us
  other arithmetic: 0.69 us -> 0 us
    unnamed x22 -> x1, local copies, waits for them, and re-layouts: 12.6 us -> 0.64 us
    reshape x1, local copies, waits for them, and re-layouts: 0.68 us -> 1.57 us  [fused_shards(): projected.reshape(cont_local, 2, out_local)]
    reshape x2 -> x0, local copies, waits for them, and re-layouts: 0.86 us -> none  [the longest x1 0.78 us: fused_shards(): residual.reshape(rows, share)]
    reshape x1, local copies, waits for them, and re-layouts: 0.63 us -> 1.39 us  [fused_shards(): layer_out.reshape(cont_local, 2, share)]
    concatenate x1 -> x0, local copies, waits for them, and re-layouts: 0.69 us -> none  [fused_shards(): jnp.concatenate([out_bias, down_bias, mlp_gain, mlp_shift, next_gain, nex...]
where the time goes in v2:
time: 56.3 us; the launch traced here: 56.1 us
  Pallas kernels  51.1 us (91%)
  local copies, waits for them, and re-layouts  4.39 us (8%)
  between operations  0.66 us (1%)
    pallas_call x1, Pallas kernels, fused_shards(): pl.pallas_call(lambda *refs: layer_kernel(sizes, *refs), out_shape=(jax.S...  51.1 us
    reshape x1, local copies, waits for them, and re-layouts, fused_shards(): projected.reshape(cont_local, 2, out_local)  1.57 us
    reshape x1, local copies, waits for them, and re-layouts, fused_shards(): layer_out.reshape(cont_local, 2, share)  1.39 us

profile of v2, /device:TPU:0, one launch (start us, length us, event | category | flops | bytes accessed | tf_op | source)
XLA Modules:
  0.0 56.1 jit_solution(3430584430255355006)
XLA Ops:
  0.6 51.1 %fused_layer.1 = (bf16[64,256]{1,0:T(8,128)(2,1)}, f32[8,128]{1,0:T(8,128)}, bf16[64,768]{1,0:T(8,128)(2,1)}) custom-call(s32[64]{0:T(128)} %refs_0_.1, s32[128]{0:T(128)} %refs_1_.1, s32[8]{0:T(128)} %refs_2_.1, s32[128]{0:T(128)} %refs_3_.1, bf16[32,3,2,512]{3,2,1,0:T(2,128)(2,1)} %bitcast.1, bf16[32,2,256]{2,1,0:T(2,128)(2,1)} %refs_5_.1, ...), custom_call_target="tpu_custom_call" | custom-call | tf_op jit(solution)/shard_map/fused_layer/pallas_call | solution.py:1007
  51.7 1.4 %reshape.12 = bf16[32,2,256]{2,1,0:T(2,128)(2,1)} reshape(bf16[64,256]{1,0:T(8,128)(2,1)} %get-tuple-element.6) | data formatting | bytes 65536 | tf_op jit(solution)/shard_map/reshape | solution.py:1101
  53.1 0.7 %slice_reduce_fusion = f32[64]{0:T(128)S(1)} fusion(f32[8,128]{1,0:T(8,128)} %get-tuple-element.7), kind=kLoop, calls=%fused_computation | loop fusion | bytes 512 | tf_op jit(solution)/shard_map/slice | solution.py:1102
  53.8 0.1 reshape_squeeze.3
  53.9 0.6 %copy.25 = f32[32,2]{0,1:T(2,128)} copy(f32[32,2]{1,0:T(8,128)S(1)} %reshape_squeeze.3) | data formatting | bytes 512
  54.5 1.6 %reshape.13 = bf16[32,2,768]{2,1,0:T(2,128)(2,1)} reshape(bf16[64,768]{1,0:T(8,128)(2,1)} %get-tuple-element.8) | data formatting | bytes 196608 | tf_op jit(solution)/shard_map/reshape | solution.py:1103

commit v3 on v2

--- a/solution.py
+++ b/solution.py
@@ -376,7 +376,7 @@
     down_hbm,
     qkv_hbm,
     layer_ref,
-    stat_ref,
+    score_ref,
     proj_ref,
     prefix_item,
     tail_item,
@@ -843,6 +843,7 @@
             normed[:, at] = (
                 (wide_buf[c].astype(f32) - center) * factor * gains[:, at] + shifts[:, at]
             ).astype(bf16)
+        return columns
 
     sums = gather(
         total.astype(bf16),
@@ -911,7 +912,6 @@
         ).wait_recv()
         total = total + d_buf[src].astype(f32)
     layer_out = total.astype(bf16)
-    layer_ref[...] = layer_out
     wide = layer_out.astype(f32)
     scores = vector(score_weight)
     score_part = scores[:, :share]
@@ -935,8 +935,7 @@
         t_send,
         t_recv,
     )
-    stat_ref[...] = sums
-    norm_into(sums, y_buf, next_gain, next_shift)
+    columns = norm_into(sums, y_buf, next_gain, next_shift)
 
     weight_copies[3].wait()
     half = pieces * piece
@@ -951,10 +950,24 @@
         copy = remote(z_stage.at[n], z_buf.at[n], z_send.at[n], z_recv.at[n], partner)
         copy.start()
         sends.append(copy)
+    layer_ref[...] = wide.reshape(layer_ref.shape).astype(bf16)
+    seat = lax.broadcasted_iota(i32, (rows, rows // 2), 1)
+    score_ref[...] = jnp.concatenate(
+        [
+            jnp.sum(
+                jnp.where(row_id == seat * 2 + u, columns[:, 2:3], 0.0), axis=0, keepdims=True
+            )
+            for u in range(2)
+        ],
+        axis=0,
+    )
     for n in range(pieces):
         own = qkv_piece(row, n) + qkv_shift[:, n * piece : (n + 1) * piece]
         remote(z_stage.at[n], z_buf.at[n], z_send.at[n], z_recv.at[n], partner).wait_recv()
-        proj_ref[:, n * piece : (n + 1) * piece] = (own + z_buf[n].astype(f32)).astype(bf16)
+        own = own + z_buf[n].astype(f32)
+        proj_ref[:, :, n * piece : (n + 1) * piece] = own.reshape(rows // 2, 2, piece).astype(
+            bf16
+        )
 
     for copy in sends:
         copy.wait_send()
@@ -963,6 +976,15 @@
             if i or k:
                 for copy in partial_copies(i, k):
                     copy.wait_send()
+
+
+def hand_out(*refs):
+    sems = refs[6]
+    copies = [pltpu.make_async_copy(refs[k], refs[3 + k], sems.at[k]) for k in range(3)]
+    for copy in copies:
+        copy.start()
+    for copy in copies:
+        copy.wait()
 
 
 def fused_shards(
@@ -996,7 +1018,7 @@
     head_width = fresh_qkv.shape[3]
     ff_local = up_weight.shape[1]
     out_local = qkv_bias.shape[0]
-    chunk = ff_local // 4
+    chunk = ff_local // 8
     piece = out_local // 2
     fresh = fresh_qkv.transpose(0, 2, 1, 3)
     one_row = (out_bias, mlp_gain, mlp_shift, up_bias, down_bias)
@@ -1004,12 +1026,12 @@
     vmem = pl.BlockSpec(memory_space=pltpu.VMEM)
     hbm = pl.BlockSpec(memory_space=pltpu.MemorySpace.HBM)
     dma = pltpu.SemaphoreType.DMA
-    layer_out, stats, projected = pl.pallas_call(
+    results = pl.pallas_call(
         lambda *refs: layer_kernel(sizes, *refs),
         out_shape=(
-            jax.ShapeDtypeStruct((rows, share), bf16),
-            jax.ShapeDtypeStruct((STAT, LANES), f32),
-            jax.ShapeDtypeStruct((rows, out_local), bf16),
+            jax.ShapeDtypeStruct((cont_local, 2, share), bf16),
+            jax.ShapeDtypeStruct((2, cont_local), f32),
+            jax.ShapeDtypeStruct((cont_local, 2, out_local), bf16),
         ),
         in_specs=[hbm] * (12 + len(one_row)),
         out_specs=(vmem, vmem, vmem),
@@ -1097,11 +1119,16 @@
         down_weight,
         qkv_weight,
     )
-    return (
-        layer_out.reshape(cont_local, 2, share),
-        stats[2, :rows].reshape(cont_local, 2),
-        projected.reshape(cont_local, 2, out_local),
-    )
+    layer_out, scores, projected = pl.pallas_call(
+        hand_out,
+        out_shape=[jax.ShapeDtypeStruct(part.shape, part.dtype) for part in results],
+        in_specs=[hbm] * 3,
+        out_specs=[hbm] * 3,
+        scratch_shapes=[dma((3,))],
+        compiler_params=pltpu.CompilerParams(vmem_limit_bytes=64 * 1024 * 1024),
+        name="hand_out",
+    )(*results)
+    return layer_out, scores.T, projected
 
 
 def shards(residual, fresh_qkv, prefix_pages, *others):

time: 56.3 us -> 57 us (1.012)
  Pallas kernels: 51.1 us -> 56.3 us
  local copies, waits for them, and re-layouts: 4.39 us -> 0 us
    pallas_call x0 -> x1, Pallas kernels: none -> 5.13 us  [fused_shards(): pl.pallas_call(hand_out, out_shape=[jax.ShapeDtypeStruct(part.shape, part...]
    reshape x2 -> x0, local copies, waits for them, and re-layouts: 2.96 us -> none  [the longest x1 1.57 us: fused_shards(): projected.reshape(cont_local, 2, out_local)]
    slice x1 -> x0, local copies, waits for them, and re-layouts: 0.69 us -> none  [fused_shards(): stats[2, :rows].reshape(cont_local, 2)]
    unnamed x1 -> x0, local copies, waits for them, and re-layouts: 0.64 us -> none
where the time goes in v3:
time: 57 us; the launch traced here: 56.9 us
  Pallas kernels  56.3 us (99%)
  between operations  0.65 us (1%)
    pallas_call x1, Pallas kernels, fused_shards(): pl.pallas_call(lambda *refs: layer_kernel(sizes, *refs), out_shape=(jax.S...  51.1 us
    pallas_call x1, Pallas kernels, fused_shards(): pl.pallas_call(hand_out, out_shape=[jax.ShapeDtypeStruct(part.shape, part...  5.13 us

profile of v3, /device:TPU:0, one launch (start us, length us, event | category | flops | bytes accessed | tf_op | source)
XLA Modules:
  0.0 56.9 jit_solution(16746872247051447536)
XLA Ops:
  0.6 51.1 %fused_layer.1 = (bf16[32,2,256]{2,1,0:T(2,128)(2,1)}, f32[2,32]{1,0:T(2,128)}, bf16[32,2,768]{2,1,0:T(2,128)(2,1)}) custom-call(s32[64]{0:T(128)} %refs_0_.1, s32[128]{0:T(128)} %refs_1_.1, s32[8]{0:T(128)} %refs_2_.1, s32[128]{0:T(128)} %refs_3_.1, bf16[32,3,2,512]{3,2,1,0:T(2,128)(2,1)} %bitcast.2, bf16[32,2,256]{2,1,0:T(2,128)(2,1)} %refs_5_.1, ...), custom_call_target="tpu_custom_call" | custom-call | tf_op jit(solution)/shard_map/fused_layer/pallas_call | solution.py:1029
  51.8 5.1 %hand_out.1 = (bf16[32,2,256]{2,1,0:T(2,128)(2,1)}, f32[2,32]{1,0:T(2,128)}, bf16[32,2,768]{2,1,0:T(2,128)(2,1)}) custom-call(bf16[32,2,256]{2,1,0:T(2,128)(2,1)} %get-tuple-element.9.refs_0_, f32[2,32]{1,0:T(2,128)} %get-tuple-element.10.refs_1_, bf16[32,2,768]{2,1,0:T(2,128)(2,1)} %get-tuple-element.11.refs_2_), custom_call_target="tpu_custom_call" | custom-call | tf_op jit(solution)/shard_map/hand_out/pallas_call | solution.py:1122

commit v4 on v3

--- a/solution.py
+++ b/solution.py
@@ -462,8 +462,8 @@
     slots, _, tokens, _ = prefix_v.shape
     tails = tail_v.shape[0]
     pair_pages, pair_tails = slots // G, tails // G
-    chunks, _, chunk = u_buf.shape
-    pieces, _, piece = z_buf.shape
+    _, chunks, _, chunk = u_buf.shape
+    _, pieces, _, piece = z_buf.shape
 
     def group_at(i):
         if isinstance(i, int) and i == 0:
@@ -760,214 +760,221 @@
     def share_of(k):
         return pl.ds(pl.multiple_of(col_at(k) * share, LANES), share)
 
-    weight_copies[0].wait()
-    for k in range(1, C):
-        t = col_at(k)
-        a_stage[k] = jnp.dot(
-            att[...], out_w[:, share_of(k)], preferred_element_type=f32
-        ).astype(bf16)
-        copy = remote(a_stage.at[k], a_buf.at[col], a_send.at[k], a_recv.at[col], (me, row, t))
+    half_rows = rows // 2
+    partner = (me, row_at(1), col)
+    per_row = chunks // R
+    last = chunks - 1
+
+    def vector(ref):
+        return ref[...].astype(f32).reshape(1, ref.shape[0])
+
+    def push(src, dst, send_sem, recv_sem, target):
+        copy = remote(src, dst, send_sem, recv_sem, target)
         copy.start()
         sends.append(copy)
 
-    def vector(ref):
-        return ref[...].astype(f32).reshape(1, ref.shape[0])
-
-    total = (
-        jnp.dot(att[...], out_w[:, share_of(0)], preferred_element_type=f32)
-        + residual[...].astype(f32).reshape(rows, share)
-        + vector(out_bias)
-    )
-    for k in range(1, C):
-        src = col_at(C - k)
-        remote(
-            a_stage.at[k], a_buf.at[src], a_send.at[k], a_recv.at[src], (me, row, src)
-        ).wait_recv()
-        total = total + a_buf[src].astype(f32)
-    hidden[...] = total
-
-    def gather(own, tile, wide_buf, wide_send, wide_recv, small_buf, small_send, small_recv):
-        small_buf[row, col] = tile
-        wide_buf[col] = own
+    def project_out(b):
+        part = att[b * half_rows : (b + 1) * half_rows, :]
+        for k in range(1, C):
+            a_stage[b, k] = jnp.dot(
+                part, out_w[:, share_of(k)], preferred_element_type=f32
+            ).astype(bf16)
+            push(
+                a_stage.at[b, k],
+                a_buf.at[b, col],
+                a_send.at[b, k],
+                a_recv.at[b, col],
+                (me, row, col_at(k)),
+            )
+        stream = residual[b * half_rows // 2 : (b + 1) * half_rows // 2].astype(f32)
+        hidden[b] = (
+            jnp.dot(part, out_w[:, share_of(0)], preferred_element_type=f32)
+            + stream.reshape(half_rows, share)
+            + vector(out_bias)
+        )
+
+    def summed(b, total, stage, buf, send, recv):
+        for k in range(1, C):
+            src = col_at(C - k)
+            remote(
+                stage.at[b, k], buf.at[b, src], send.at[b, k], recv.at[b, src], (me, row, src)
+            ).wait_recv()
+            total = total + buf[b, src].astype(f32)
+        return total
+
+    def gather_start(b, own, parts, wide_buf, wide_send, wide_recv, small_buf, small_send, small_recv):
+        wide_buf[b, col] = own
+        small_buf[b, row, col] = columns_to_tile(
+            [jnp.sum(part, axis=1, keepdims=True) for part in parts]
+        )
         for k in range(R):
             for j in range(C):
                 if k or j:
-                    copy = remote(
-                        small_buf.at[row, col],
-                        small_buf.at[row, col],
-                        small_send.at[k, j],
-                        small_recv.at[row, col],
+                    push(
+                        small_buf.at[b, row, col],
+                        small_buf.at[b, row, col],
+                        small_send.at[b, k, j],
+                        small_recv.at[b, row, col],
                         (me, row_at(k), col_at(j)),
                     )
-                    copy.start()
-                    sends.append(copy)
         for j in range(1, C):
-            copy = remote(
-                wide_buf.at[col],
-                wide_buf.at[col],
-                wide_send.at[j],
-                wide_recv.at[col],
+            push(
+                wide_buf.at[b, col],
+                wide_buf.at[b, col],
+                wide_send.at[b, j],
+                wide_recv.at[b, col],
                 (me, row, col_at(j)),
             )
-            copy.start()
-            sends.append(copy)
+
+    def gather_norm(
+        b, gain, shift, wide_buf, wide_send, wide_recv, small_buf, small_send, small_recv
+    ):
         for k in range(R):
             for j in range(C):
                 if k or j:
                     r, c = row_at(k), col_at(j)
                     remote(
-                        small_buf.at[row, col],
-                        small_buf.at[r, c],
-                        small_send.at[k, j],
-                        small_recv.at[r, c],
+                        small_buf.at[b, row, col],
+                        small_buf.at[b, r, c],
+                        small_send.at[b, k, j],
+                        small_recv.at[b, r, c],
                         (me, r, c),
                     ).wait_recv()
-        sums = small_buf[0, 0]
+        sums = small_buf[b, 0, 0]
         for k in range(1, R * C):
-            sums = sums + small_buf[k // C, k % C]
-        for j in range(1, C):
-            c = col_at(j)
-            remote(
-                wide_buf.at[col], wide_buf.at[c], wide_send.at[j], wide_recv.at[c], (me, row, c)
-            ).wait_recv()
-        return sums
-
-    def norm_into(sums, wide_buf, gain, shift):
-        columns = tile_to_columns(sums, rows)
+            sums = sums + small_buf[b, k // C, k % C]
+        columns = tile_to_columns(sums, half_rows)
         center = columns[:, 0:1] / D
         spread = columns[:, 1:2] / D - center * center
         factor = lax.rsqrt(spread + norm_eps)
         gains, shifts = vector(gain), vector(shift)
+        for j in range(1, C):
+            c = col_at(j)
+            remote(
+                wide_buf.at[b, col],
+                wide_buf.at[b, c],
+                wide_send.at[b, j],
+                wide_recv.at[b, c],
+                (me, row, c),
+            ).wait_recv()
         for c in range(C):
             at = slice(c * share, (c + 1) * share)
-            normed[:, at] = (
-                (wide_buf[c].astype(f32) - center) * factor * gains[:, at] + shifts[:, at]
+            normed[b, :, at] = (
+                (wide_buf[b, c].astype(f32) - center) * factor * gains[:, at] + shifts[:, at]
             ).astype(bf16)
         return columns
 
-    sums = gather(
-        total.astype(bf16),
-        columns_to_tile(
-            [
-                jnp.sum(total, axis=1, keepdims=True),
-                jnp.sum(total * total, axis=1, keepdims=True),
-            ]
-        ),
-        x_buf,
-        x_send,
-        x_recv,
-        s_buf,
-        s_send,
-        s_recv,
-    )
-    norm_into(sums, x_buf, mlp_gain, mlp_shift)
-
-    partner = (me, row_at(1), col)
+    first_gather = (x_buf, x_send, x_recv, s_buf, s_send, s_recv)
+    second_gather = (y_buf, y_send, y_recv, t_buf, t_send, t_recv)
+
+    def up_copy(b, n):
+        return (u_stage.at[b, n], u_buf.at[b, n], u_send.at[b, n], u_recv.at[b, n], partner)
+
+    def project_up(b):
+        up_shift = vector(up_bias)
+        for n in range(chunks):
+            part = jnp.dot(
+                normed[b], up_w[:, n * chunk : (n + 1) * chunk], preferred_element_type=f32
+            )
+            mine = jnp.where(jnp.full((1, chunk), row, i32) == n // per_row, 1.0, 0.0)
+            spot = n % per_row
+            part = part + mine * up_shift[:, spot * chunk : (spot + 1) * chunk]
+            u_own[b, n] = part
+            u_stage[b, n] = part.astype(bf16)
+            push(*up_copy(b, n))
+
+    def project_down(b):
+        for n in range(chunks):
+            remote(*up_copy(b, n)).wait_recv()
+            v = u_own[b, n] + u_buf[b, n].astype(f32)
+            gelu = (
+                0.5 * v * (1.0 + jnp.tanh(0.7978845608 * (v + 0.044715 * (v * v * v))))
+            ).astype(bf16)
+            if n < last:
+                term = jnp.dot(
+                    gelu, down_w[n * chunk : (n + 1) * chunk, :], preferred_element_type=f32
+                )
+                acc[b] = term if n == 0 else acc[b] + term
+
+        def down_for(k):
+            return acc[b, :, share_of(k)] + jnp.dot(
+                gelu, down_w[last * chunk :, share_of(k)], preferred_element_type=f32
+            )
+
+        for k in range(1, C):
+            d_stage[b, k] = down_for(k).astype(bf16)
+            push(
+                d_stage.at[b, k],
+                d_buf.at[b, col],
+                d_send.at[b, k],
+                d_recv.at[b, col],
+                (me, row, col_at(k)),
+            )
+        hidden[b] = hidden[b] + down_for(0) + vector(down_bias)
+
+    half = pieces * piece
+
+    def qkv_piece(b, r, n):
+        at = pl.ds(pl.multiple_of(r * half + n * piece, LANES), piece)
+        return jnp.dot(normed[b], qkv_w[:, at], preferred_element_type=f32)
+
+    def z_copy(b, n):
+        return (z_stage.at[b, n], z_buf.at[b, n], z_send.at[b, n], z_recv.at[b, n], partner)
+
+    weight_copies[0].wait()
+    for b in range(2):
+        project_out(b)
+    for b in range(2):
+        total = summed(b, hidden[b], a_stage, a_buf, a_send, a_recv)
+        hidden[b] = total
+        gather_start(b, total.astype(bf16), [total, total * total], *first_gather)
     weight_copies[1].wait()
-    per_row = chunks // R
-    up_shift = vector(up_bias)
-    for n in range(chunks):
-        part = jnp.dot(
-            normed[...], up_w[:, n * chunk : (n + 1) * chunk], preferred_element_type=f32
-        )
-        mine = jnp.where(jnp.full((1, chunk), row, i32) == n // per_row, 1.0, 0.0)
-        part = part + mine * up_shift[:, (n % per_row) * chunk : (n % per_row + 1) * chunk]
-        u_own[n] = part
-        u_stage[n] = part.astype(bf16)
-        copy = remote(u_stage.at[n], u_buf.at[n], u_send.at[n], u_recv.at[n], partner)
-        copy.start()
-        sends.append(copy)
-
+    for b in range(2):
+        gather_norm(b, mlp_gain, mlp_shift, *first_gather)
+        project_up(b)
     weight_copies[2].wait()
-    last = chunks - 1
-    for n in range(chunks):
-        remote(u_stage.at[n], u_buf.at[n], u_send.at[n], u_recv.at[n], partner).wait_recv()
-        v = u_own[n] + u_buf[n].astype(f32)
-        gelu = (0.5 * v * (1.0 + jnp.tanh(0.7978845608 * (v + 0.044715 * (v * v * v))))).astype(
-            bf16
-        )
-        if n < last:
-            term = jnp.dot(
-                gelu, down_w[n * chunk : (n + 1) * chunk, :], preferred_element_type=f32
-            )
-            acc[...] = term if n == 0 else acc[...] + term
-
-    def down_for(k):
-        return acc[:, share_of(k)] + jnp.dot(
-            gelu, down_w[last * chunk :, share_of(k)], preferred_element_type=f32
-        )
-
-    for k in range(1, C):
-        d_stage[k] = down_for(k).astype(bf16)
-        copy = remote(
-            d_stage.at[k], d_buf.at[col], d_send.at[k], d_recv.at[col], (me, row, col_at(k))
-        )
-        copy.start()
-        sends.append(copy)
-    total = down_for(0) + hidden[...] + vector(down_bias)
-    for k in range(1, C):
-        src = col_at(C - k)
-        remote(
-            d_stage.at[k], d_buf.at[src], d_send.at[k], d_recv.at[src], (me, row, src)
-        ).wait_recv()
-        total = total + d_buf[src].astype(f32)
-    layer_out = total.astype(bf16)
-    wide = layer_out.astype(f32)
+    for b in range(2):
+        project_down(b)
+
     scores = vector(score_weight)
     score_part = scores[:, :share]
     for c in range(1, C):
         score_part = jnp.where(
             jnp.full((1, share), col, i32) == c, scores[:, c * share : (c + 1) * share], score_part
         )
-    sums = gather(
-        layer_out,
-        columns_to_tile(
-            [
-                jnp.sum(wide, axis=1, keepdims=True),
-                jnp.sum(wide * wide, axis=1, keepdims=True),
-                jnp.sum(wide * score_part, axis=1, keepdims=True),
-            ]
-        ),
-        y_buf,
-        y_send,
-        y_recv,
-        t_buf,
-        t_send,
-        t_recv,
-    )
-    columns = norm_into(sums, y_buf, next_gain, next_shift)
-
+    quarter = half_rows // 2
+    for b in range(2):
+        layer_out = summed(b, hidden[b], d_stage, d_buf, d_send, d_recv).astype(bf16)
+        wide = layer_out.astype(f32)
+        gather_start(b, layer_out, [wide, wide * wide, wide * score_part], *second_gather)
+        layer_ref[b * quarter : (b + 1) * quarter] = wide.reshape(quarter, 2, share).astype(bf16)
     weight_copies[3].wait()
-    half = pieces * piece
-    qkv_shift = vector(qkv_bias)
-
-    def qkv_piece(r, n):
-        at = pl.ds(pl.multiple_of(r * half + n * piece, LANES), piece)
-        return jnp.dot(normed[...], qkv_w[:, at], preferred_element_type=f32)
-
-    for n in range(pieces):
-        z_stage[n] = qkv_piece(row_at(1), n).astype(bf16)
-        copy = remote(z_stage.at[n], z_buf.at[n], z_send.at[n], z_recv.at[n], partner)
-        copy.start()
-        sends.append(copy)
-    layer_ref[...] = wide.reshape(layer_ref.shape).astype(bf16)
+    score_columns = []
+    for b in range(2):
+        columns = gather_norm(b, next_gain, next_shift, *second_gather)
+        score_columns.append(columns[:, 2:3])
+        for n in range(pieces):
+            z_stage[b, n] = qkv_piece(b, row_at(1), n).astype(bf16)
+            push(*z_copy(b, n))
     seat = lax.broadcasted_iota(i32, (rows, rows // 2), 1)
+    score_column = jnp.concatenate(score_columns, axis=0)
     score_ref[...] = jnp.concatenate(
         [
-            jnp.sum(
-                jnp.where(row_id == seat * 2 + u, columns[:, 2:3], 0.0), axis=0, keepdims=True
-            )
+            jnp.sum(jnp.where(row_id == seat * 2 + u, score_column, 0.0), axis=0, keepdims=True)
             for u in range(2)
         ],
         axis=0,
     )
-    for n in range(pieces):
-        own = qkv_piece(row, n) + qkv_shift[:, n * piece : (n + 1) * piece]
-        remote(z_stage.at[n], z_buf.at[n], z_send.at[n], z_recv.at[n], partner).wait_recv()
-        own = own + z_buf[n].astype(f32)
-        proj_ref[:, :, n * piece : (n + 1) * piece] = own.reshape(rows // 2, 2, piece).astype(
-            bf16
-        )
+    qkv_shift = vector(qkv_bias)
+    for b in range(2):
+        for n in range(pieces):
+            at = slice(n * piece, (n + 1) * piece)
+            own = qkv_piece(b, row, n) + qkv_shift[:, at]
+            remote(*z_copy(b, n)).wait_recv()
+            own = own + z_buf[b, n].astype(f32)
+            proj_ref[b * quarter : (b + 1) * quarter, :, at] = own.reshape(
+                quarter, 2, piece
+            ).astype(bf16)
 
     for copy in sends:
         copy.wait_send()
@@ -979,12 +986,8 @@
 
 
 def hand_out(*refs):
-    sems = refs[6]
-    copies = [pltpu.make_async_copy(refs[k], refs[3 + k], sems.at[k]) for k in range(3)]
-    for copy in copies:
-        copy.start()
-    for copy in copies:
-        copy.wait()
+    for k in range(3):
+        refs[3 + k][...] = refs[k][...]
 
 
 def fused_shards(
@@ -1015,11 +1018,12 @@
     f32, bf16 = jnp.float32, jnp.bfloat16
     cont_local, _, share = residual.shape
     rows = cont_local * 2
+    half = rows // 2
     head_width = fresh_qkv.shape[3]
     ff_local = up_weight.shape[1]
     out_local = qkv_bias.shape[0]
-    chunk = ff_local // 8
-    piece = out_local // 2
+    chunk = ff_local // 4
+    piece = out_local
     fresh = fresh_qkv.transpose(0, 2, 1, 3)
     one_row = (out_bias, mlp_gain, mlp_shift, up_bias, down_bias)
     one_row = one_row + (next_gain, next_shift, score_weight, qkv_bias)
@@ -1059,22 +1063,22 @@
             pltpu.VMEM((G, R, rows, head_width), bf16),
             pltpu.VMEM((G, R, STAT, LANES), f32),
             pltpu.VMEM((rows, head_width), bf16),
-            pltpu.VMEM((C, rows, share), bf16),
-            pltpu.VMEM((C, rows, share), bf16),
-            pltpu.VMEM((rows, share), f32),
-            pltpu.VMEM((C, rows, share), bf16),
-            pltpu.VMEM((R, C, STAT, LANES), f32),
-            pltpu.VMEM((rows, C * share), bf16),
-            pltpu.VMEM((ff_local // chunk, rows, chunk), f32),
-            pltpu.VMEM((ff_local // chunk, rows, chunk), bf16),
-            pltpu.VMEM((ff_local // chunk, rows, chunk), bf16),
-            pltpu.VMEM((rows, C * share), f32),
-            pltpu.VMEM((C, rows, share), bf16),
-            pltpu.VMEM((C, rows, share), bf16),
-            pltpu.VMEM((C, rows, share), bf16),
-            pltpu.VMEM((R, C, STAT, LANES), f32),
-            pltpu.VMEM((out_local // piece, rows, piece), bf16),
-            pltpu.VMEM((out_local // piece, rows, piece), bf16),
+            pltpu.VMEM((2, C, half, share), bf16),
+            pltpu.VMEM((2, C, half, share), bf16),
+            pltpu.VMEM((2, half, share), f32),
+            pltpu.VMEM((2, C, half, share), bf16),
+            pltpu.VMEM((2, R, C, STAT, LANES), f32),
+            pltpu.VMEM((2, half, C * share), bf16),
+            pltpu.VMEM((2, ff_local // chunk, half, chunk), f32),
+            pltpu.VMEM((2, ff_local // chunk, half, chunk), bf16),
+            pltpu.VMEM((2, ff_local // chunk, half, chunk), bf16),
+            pltpu.VMEM((2, half, C * share), f32),
+            pltpu.VMEM((2, C, half, share), bf16),
+            pltpu.VMEM((2, C, half, share), bf16),
+            pltpu.VMEM((2, C, half, share), bf16),
+            pltpu.VMEM((2, R, C, STAT, LANES), f32),
+            pltpu.VMEM((2, out_local // piece, half, piece), bf16),
+            pltpu.VMEM((2, out_local // piece, half, piece), bf16),
             dma((G, 2)),
             dma((4,)),
             dma((G,)),
@@ -1083,22 +1087,22 @@
             dma((G, R)),
             dma((G, R)),
             dma((G, R)),
-            dma((C,)),
-            dma((C,)),
-            dma((C,)),
-            dma((C,)),
-            dma((R, C)),
-            dma((R, C)),
-            dma((ff_local // chunk,)),
-            dma((ff_local // chunk,)),
-            dma((C,)),
-            dma((C,)),
-            dma((C,)),
-            dma((C,)),
-            dma((R, C)),
-            dma((R, C)),
-            dma((out_local // piece,)),
-            dma((out_local // piece,)),
+            dma((2, C)),
+            dma((2, C)),
+            dma((2, C)),
+            dma((2, C)),
+            dma((2, R, C)),
+            dma((2, R, C)),
+            dma((2, ff_local // chunk)),
+            dma((2, ff_local // chunk)),
+            dma((2, C)),
+            dma((2, C)),
+            dma((2, C)),
+            dma((2, C)),
+            dma((2, R, C)),
+            dma((2, R, C)),
+            dma((2, out_local // piece)),
+            dma((2, out_local // piece)),
         ],
         compiler_params=pltpu.CompilerParams(
             collective_id=0, has_side_effects=True, vmem_limit_bytes=64 * 1024 * 1024
@@ -1122,9 +1126,8 @@
     layer_out, scores, projected = pl.pallas_call(
         hand_out,
         out_shape=[jax.ShapeDtypeStruct(part.shape, part.dtype) for part in results],
-        in_specs=[hbm] * 3,
-        out_specs=[hbm] * 3,
-        scratch_shapes=[dma((3,))],
+        in_specs=[vmem] * 3,
+        out_specs=[vmem] * 3,
         compiler_params=pltpu.CompilerParams(vmem_limit_bytes=64 * 1024 * 1024),
         name="hand_out",
     )(*results)

time: 57 us -> 51.3 us (0.90)
  Pallas kernels: 56.3 us -> 50.5 us
    pallas_call x1, Pallas kernels: 5.13 us -> 1.58 us  [fused_shards(): pl.pallas_call(hand_out, out_shape=[jax.ShapeDtypeStruct(part.shape, part...]
    pallas_call x1, Pallas kernels: 51.1 us -> 49 us  [fused_shards(): pl.pallas_call(lambda *refs: layer_kernel(sizes, *refs), out_shape=(jax.S...]
where the time goes in v4:
time: 51.3 us; the launch traced here: 51.2 us
  Pallas kernels  50.5 us (98%)
  between operations  0.65 us (1%)
    pallas_call x1, Pallas kernels, fused_shards(): pl.pallas_call(lambda *refs: layer_kernel(sizes, *refs), out_shape=(jax.S...  49 us
    pallas_call x1, Pallas kernels, fused_shards(): pl.pallas_call(hand_out, out_shape=[jax.ShapeDtypeStruct(part.shape, part...  1.58 us

profile of v4, /device:TPU:0, one launch (start us, length us, event | category | flops | bytes accessed | tf_op | source)
XLA Modules:
  0.0 51.2 jit_solution(15898876459758131828)
XLA Ops:
  0.6 49.0 %fused_layer.1 = (bf16[32,2,256]{2,1,0:T(2,128)(2,1)}, f32[2,32]{1,0:T(2,128)}, bf16[32,2,768]{2,1,0:T(2,128)(2,1)}) custom-call(s32[64]{0:T(128)} %refs_0_.1, s32[128]{0:T(128)} %refs_1_.1, s32[8]{0:T(128)} %refs_2_.1, s32[128]{0:T(128)} %refs_3_.1, bf16[32,3,2,512]{3,2,1,0:T(2,128)(2,1)} %bitcast.2, bf16[32,2,256]{2,1,0:T(2,128)(2,1)} %refs_5_.1, ...), custom_call_target="tpu_custom_call" | custom-call | tf_op jit(solution)/shard_map/fused_layer/pallas_call | solution.py:1033
  49.6 1.6 %hand_out.1 = (bf16[32,2,256]{2,1,0:T(2,128)(2,1)}, f32[2,32]{1,0:T(2,128)}, bf16[32,2,768]{2,1,0:T(2,128)(2,1)}) custom-call(bf16[32,2,256]{2,1,0:T(2,128)(2,1)} %get-tuple-element.9.refs_0_, f32[2,32]{1,0:T(2,128)} %get-tuple-element.10.refs_1_, bf16[32,2,768]{2,1,0:T(2,128)(2,1)} %get-tuple-element.11.refs_2_), custom_call_target="tpu_custom_call" | custom-call | tf_op jit(solution)/shard_map/hand_out/pallas_call | solution.py:1126

commit v5 on v4

--- a/solution.py
+++ b/solution.py
@@ -350,6 +350,20 @@
     if have < LANES:
         tile = jnp.concatenate([tile, jnp.zeros((LANES - have, LANES), jnp.float32)], axis=0)
     return jnp.transpose(tile)[:rows]
+
+
+def split_level(tile, width):
+    high = tile.astype(jnp.bfloat16).astype(jnp.float32)
+    middle = (tile - high).astype(jnp.bfloat16).astype(jnp.float32)
+    parts = [high, middle, tile - high - middle]
+    parts += [jnp.zeros_like(tile)] * (width // LANES - len(parts))
+    block = jnp.concatenate(parts, axis=1)
+    return jnp.concatenate([block, jnp.zeros_like(block)], axis=0).astype(jnp.bfloat16)
+
+
+def join_level(block):
+    parts = block.astype(jnp.float32)[:STAT]
+    return parts[:, :LANES] + parts[:, LANES : 2 * LANES] + parts[:, 2 * LANES : 3 * LANES]
 
 
 def layer_kernel(
@@ -405,9 +419,7 @@
     qkv_w,
     q_buf,
     p_stage,
-    l_stage,
     p_buf,
-    l_buf,
     att,
     a_stage,
     a_buf,
@@ -431,8 +443,6 @@
     q_recv,
     p_send,
     p_recv,
-    l_send,
-    l_recv,
     a_send,
     a_recv,
     x_send,
@@ -683,43 +693,37 @@
             out = jnp.dot(w_one.astype(bf16), values, preferred_element_type=f32) + jnp.dot(
                 w_two.astype(bf16), tail_values, preferred_element_type=f32
             )
-            p_stage[g, :, hs] = (out / total).astype(bf16)
+            p_stage[g, :rows, hs] = (out / total).astype(bf16)
             levels.append(top + jnp.log(total))
-        l_stage[g] = columns_to_tile(levels)
-
-    def partial_copies(i, k):
+        p_stage[g, rows:, :] = split_level(columns_to_tile(levels), heads * HD)
+
+    def partial_copy(i, k):
         g = group_at(i)
-        target = (g, row_at(k), col)
-        return (
-            remote(
-                p_stage.at[g], p_buf.at[me, row], p_send.at[g, k], p_recv.at[me, row], target
-            ),
-            remote(
-                l_stage.at[g], l_buf.at[me, row], l_send.at[g, k], l_recv.at[me, row], target
-            ),
+        return remote(
+            p_stage.at[g],
+            p_buf.at[me, row],
+            p_send.at[g, k],
+            p_recv.at[me, row],
+            (g, row_at(k), col),
         )
 
-    def partial_arrivals(i, k):
+    def partial_arrival(i, k):
         g, r = group_at(i), row_at(k)
-        return (
-            remote(p_stage.at[g], p_buf.at[g, r], p_send.at[g, k], p_recv.at[g, r], (g, r, col)),
-            remote(l_stage.at[g], l_buf.at[g, r], l_send.at[g, k], l_recv.at[g, r], (g, r, col)),
+        return remote(
+            p_stage.at[g], p_buf.at[g, r], p_send.at[g, k], p_recv.at[g, r], (g, r, col)
         )
 
     attend(0)
     for k in range(1, R):
-        for copy in partial_copies(0, k):
-            copy.start()
+        partial_copy(0, k).start()
     p_buf[me, row] = p_stage[me]
-    l_buf[me, row] = l_stage[me]
 
     def next_group(i, carry):
         g = group_at(i)
         remote(fresh.at[0], q_buf.at[g], q_send.at[i], q_recv.at[g], (g, row, col)).wait_recv()
         attend(i)
         for k in range(R):
-            for copy in partial_copies(i, k):
-                copy.start()
+            partial_copy(i, k).start()
         return carry
 
     lax.fori_loop(1, G, next_group, 0)
@@ -727,10 +731,9 @@
     for i in range(G):
         for k in range(R):
             if i or k:
-                for copy in partial_arrivals(i, k):
-                    copy.wait_recv()
-
-    peers = [l_buf[g, r] for g in range(G) for r in range(R)] + [new_level]
+                partial_arrival(i, k).wait_recv()
+
+    peers = [join_level(p_buf[g, r, rows:, :]) for g in range(G) for r in range(R)] + [new_level]
     peak = peers[0]
     for level in peers[1:]:
         peak = jnp.maximum(peak, level)
@@ -749,13 +752,16 @@
         at = spot * STAT + h
         return groups_of_tiles[block][:, at : at + 1]
 
-    for h in range(heads):
-        hs = slice(h * HD, (h + 1) * HD)
-        joined = weight_of(G * R, h) * new_out[:, hs]
-        for g in range(G):
-            for r in range(R):
-                joined = joined + weight_of(g * R + r, h) * p_buf[g, r, :, hs].astype(f32)
-        att[:, hs] = joined.astype(bf16)
+    def merge(b):
+        part = slice(b * half_rows, (b + 1) * half_rows)
+        for h in range(heads):
+            hs = slice(h * HD, (h + 1) * HD)
+            joined = weight_of(G * R, h)[part] * new_out[part, hs]
+            for g in range(G):
+                for r in range(R):
+                    share_now = weight_of(g * R + r, h)[part]
+                    joined = joined + share_now * p_buf[g, r, part, hs].astype(f32)
+            att[part, hs] = joined.astype(bf16)
 
     def share_of(k):
         return pl.ds(pl.multiple_of(col_at(k) * share, LANES), share)
@@ -923,6 +929,7 @@
 
     weight_copies[0].wait()
     for b in range(2):
+        merge(b)
         project_out(b)
     for b in range(2):
         total = summed(b, hidden[b], a_stage, a_buf, a_send, a_recv)
@@ -981,8 +988,7 @@
     for i in range(G):
         for k in range(R):
             if i or k:
-                for copy in partial_copies(i, k):
-                    copy.wait_send()
+                partial_copy(i, k).wait_send()
 
 
 def hand_out(*refs):
@@ -1058,10 +1064,8 @@
             pltpu.VMEM(down_weight.shape, bf16),
             pltpu.VMEM(qkv_weight.shape, bf16),
             pltpu.VMEM((G, rows, head_width), bf16),
-            pltpu.VMEM((G, rows, head_width), bf16),
-            pltpu.VMEM((G, STAT, LANES), f32),
-            pltpu.VMEM((G, R, rows, head_width), bf16),
-            pltpu.VMEM((G, R, STAT, LANES), f32),
+            pltpu.VMEM((G, rows + 2 * STAT, head_width), bf16),
+            pltpu.VMEM((G, R, rows + 2 * STAT, head_width), bf16),
             pltpu.VMEM((rows, head_width), bf16),
             pltpu.VMEM((2, C, half, share), bf16),
             pltpu.VMEM((2, C, half, share), bf16),
@@ -1083,8 +1087,6 @@
             dma((4,)),
             dma((G,)),
             dma((G,)),
-            dma((G, R)),
-            dma((G, R)),
             dma((G, R)),
             dma((G, R)),
             dma((2, C)),
@@ -1136,8 +1138,9 @@
 
 def shards(residual, fresh_qkv, prefix_pages, *others):
     sizes = {axis: lax.axis_size(axis) for axis in ("pages", "row", "col")}
-    share, tokens = residual.shape[2], prefix_pages.shape[2]
-    if sizes["row"] == 2 and sizes["pages"] % 2 == 0 and share % LANES == 0 and tokens % 16 == 0:
+    share, tokens, width = residual.shape[2], prefix_pages.shape[2], fresh_qkv.shape[3]
+    whole = share % LANES == 0 and tokens % 16 == 0 and width >= 3 * LANES
+    if sizes["row"] == 2 and sizes["pages"] % 2 == 0 and whole:
         return fused_shards(sizes, residual, fresh_qkv, prefix_pages, *others)
     return plain_shards(residual, fresh_qkv, prefix_pages, *others)
 

time: 51.3 us -> 51.7 us (level)
  no operation moved by 1% of the time
where the time goes in v5:
time: 51.7 us; the launch traced here: 51.5 us
  Pallas kernels  50.9 us (98%)
  between operations  0.65 us (1%)
    pallas_call x1, Pallas kernels, fused_shards(): pl.pallas_call(lambda *refs: layer_kernel(sizes, *refs), out_shape=(jax.S...  49.3 us
    pallas_call x1, Pallas kernels, fused_shards(): pl.pallas_call(hand_out, out_shape=[jax.ShapeDtypeStruct(part.shape, part...  1.58 us

profile of v5, /device:TPU:0, one launch (start us, length us, event | category | flops | bytes accessed | tf_op | source)
XLA Modules:
  0.0 51.5 jit_solution(6428143381187658681)
XLA Ops:
  0.6 49.3 %fused_layer.1 = (bf16[32,2,256]{2,1,0:T(2,128)(2,1)}, f32[2,32]{1,0:T(2,128)}, bf16[32,2,768]{2,1,0:T(2,128)(2,1)}) custom-call(s32[64]{0:T(128)} %refs_0_.1, s32[128]{0:T(128)} %refs_1_.1, s32[8]{0:T(128)} %refs_2_.1, s32[128]{0:T(128)} %refs_3_.1, bf16[32,3,2,512]{3,2,1,0:T(2,128)(2,1)} %bitcast.2, bf16[32,2,256]{2,1,0:T(2,128)(2,1)} %refs_5_.1, ...), custom_call_target="tpu_custom_call" | custom-call | tf_op jit(solution)/shard_map/fused_layer/pallas_call | solution.py:1039
  49.9 1.6 %hand_out.1 = (bf16[32,2,256]{2,1,0:T(2,128)(2,1)}, f32[2,32]{1,0:T(2,128)}, bf16[32,2,768]{2,1,0:T(2,128)(2,1)}) custom-call(bf16[32,2,256]{2,1,0:T(2,128)(2,1)} %get-tuple-element.9.refs_0_, f32[2,32]{1,0:T(2,128)} %get-tuple-element.10.refs_1_, bf16[32,2,768]{2,1,0:T(2,128)(2,1)} %get-tuple-element.11.refs_2_), custom_call_target="tpu_custom_call" | custom-call | tf_op jit(solution)/shard_map/hand_out/pallas_call | solution.py:1128

commit v6 on v4

--- a/solution.py
+++ b/solution.py
@@ -655,36 +655,48 @@
 
         pre = pl.ds(g * pair_pages, pair_pages)
         tai = pl.ds(g * pair_tails, pair_tails)
-        levels = []
-        for h in range(heads):
-            hs = slice(h * HD, (h + 1) * HD)
+        spans = [slice(h * HD, (h + 1) * HD) for h in range(heads)]
+        scored = []
+        for h, hs in enumerate(spans):
             query = q_buf[g, :, hs]
             keys = prefix_v[pre, 0, :, hs].reshape(pair_pages * tokens, HD)
             tail_keys = tail_v[tai, 0, :, hs].reshape(pair_tails * tokens, HD)
-            s_one = (
-                lax.dot_general(query, keys, contract_last, preferred_element_type=f32) * scale
-                + slope_row(h, pair_pages * tokens) * prefix_gap
+            s_one = lax.dot_general(query, keys, contract_last, preferred_element_type=f32)
+            s_two = lax.dot_general(query, tail_keys, contract_last, preferred_element_type=f32)
+            scored.append(
+                (
+                    s_one * scale + slope_row(h, pair_pages * tokens) * prefix_gap,
+                    s_two * scale + slope_row(h, pair_tails * tokens) * tail_gap,
+                )
             )
-            s_two = (
-                lax.dot_general(query, tail_keys, contract_last, preferred_element_type=f32)
-                * scale
-                + slope_row(h, pair_tails * tokens) * tail_gap
+        tops = [
+            jnp.maximum(
+                jnp.maximum(
+                    jnp.max(s_one, axis=1, keepdims=True), jnp.max(s_two, axis=1, keepdims=True)
+                ),
+                empty_floor,
             )
-            top = jnp.maximum(
-                jnp.max(s_one, axis=1, keepdims=True), jnp.max(s_two, axis=1, keepdims=True)
+            for s_one, s_two in scored
+        ]
+        weighed = [
+            (jnp.exp(s_one - top), jnp.exp(s_two - top))
+            for (s_one, s_two), top in zip(scored, tops)
+        ]
+        totals = [
+            jnp.maximum(
+                jnp.sum(w_one, axis=1, keepdims=True) + jnp.sum(w_two, axis=1, keepdims=True),
+                1e-30,
             )
-            top = jnp.maximum(top, empty_floor)
-            w_one = jnp.exp(s_one - top)
-            w_two = jnp.exp(s_two - top)
-            total = jnp.sum(w_one, axis=1, keepdims=True) + jnp.sum(w_two, axis=1, keepdims=True)
-            total = jnp.maximum(total, 1e-30)
+            for w_one, w_two in weighed
+        ]
+        for hs, (w_one, w_two), total in zip(spans, weighed, totals):
             values = prefix_v[pre, 1, :, hs].reshape(pair_pages * tokens, HD)
             tail_values = tail_v[tai, 1, :, hs].reshape(pair_tails * tokens, HD)
             out = jnp.dot(w_one.astype(bf16), values, preferred_element_type=f32) + jnp.dot(
                 w_two.astype(bf16), tail_values, preferred_element_type=f32
             )
-            p_stage[g, :, hs] = (out / total).astype(bf16)
-            levels.append(top + jnp.log(total))
+            p_stage[g, :, hs] = (out * (1.0 / total)).astype(bf16)
+        levels = [top + jnp.log(total) for top, total in zip(tops, totals)]
         l_stage[g] = columns_to_tile(levels)
 
     def partial_copies(i, k):

time: 51.3 us -> 50.5 us (0.984)
  Pallas kernels: 50.5 us -> 49.7 us
    pallas_call x1, Pallas kernels: 49 us -> 48.1 us  [fused_shards(): pl.pallas_call(lambda *refs: layer_kernel(sizes, *refs), out_shape=(jax.S...]
where the time goes in v6:
time: 50.5 us; the launch traced here: 50.3 us
  Pallas kernels  49.7 us (98%)
  between operations  0.65 us (1%)
    pallas_call x1, Pallas kernels, fused_shards(): pl.pallas_call(lambda *refs: layer_kernel(sizes, *refs), out_shape=(jax.S...  48.1 us
    pallas_call x1, Pallas kernels, fused_shards(): pl.pallas_call(hand_out, out_shape=[jax.ShapeDtypeStruct(part.shape, part...  1.58 us

profile of v6, /device:TPU:0, one launch (start us, length us, event | category | flops | bytes accessed | tf_op | source)
XLA Modules:
  0.0 50.3 jit_solution(9682264516553406919)
XLA Ops:
  0.6 48.1 %fused_layer.1 = (bf16[32,2,256]{2,1,0:T(2,128)(2,1)}, f32[2,32]{1,0:T(2,128)}, bf16[32,2,768]{2,1,0:T(2,128)(2,1)}) custom-call(s32[64]{0:T(128)} %refs_0_.1, s32[128]{0:T(128)} %refs_1_.1, s32[8]{0:T(128)} %refs_2_.1, s32[128]{0:T(128)} %refs_3_.1, bf16[32,3,2,512]{3,2,1,0:T(2,128)(2,1)} %bitcast.2, bf16[32,2,256]{2,1,0:T(2,128)(2,1)} %refs_5_.1, ...), custom_call_target="tpu_custom_call" | custom-call | tf_op jit(solution)/shard_map/fused_layer/pallas_call | solution.py:1045
  48.7 1.6 %hand_out.1 = (bf16[32,2,256]{2,1,0:T(2,128)(2,1)}, f32[2,32]{1,0:T(2,128)}, bf16[32,2,768]{2,1,0:T(2,128)(2,1)}) custom-call(bf16[32,2,256]{2,1,0:T(2,128)(2,1)} %get-tuple-element.9.refs_0_, f32[2,32]{1,0:T(2,128)} %get-tuple-element.10.refs_1_, bf16[32,2,768]{2,1,0:T(2,128)(2,1)} %get-tuple-element.11.refs_2_), custom_call_target="tpu_custom_call" | custom-call | tf_op jit(solution)/shard_map/hand_out/pallas_call | solution.py:1138
